TPU v7x, 32 devices: a whole 2x2x4 slice. The times are simulated.
32 devices in a mesh: gx: 4 (over x, core), gy: 8 (over z, y).
Axes of the slice: x: 2, y: 2, z: 4, core: 2. Of those that a mesh axis runs over, the one named last changes fastest.
Arguments:
- parent_fields: float32 [5, 4, 192, 3072], P(None, None, 'gx', 'gy'), may hold values from -6 to 6
- parent_velocity: float32 [2, 4, 192, 3072], P(None, None, 'gx', 'gy'), may hold values from -0.3 to 0.3
- parent_mixing: float32 [4, 192, 3072], P(None, 'gx', 'gy'), may hold values from 0.01 to 0.1
- nest_fields: float32 [5, 4, 192, 3072], P(None, None, 'gx', 'gy'), may hold values from -6 to 6
- nest_velocity: float32 [2, 4, 192, 3072], P(None, None, 'gx', 'gy'), may hold values from -0.3 to 0.3
- nest_mixing: float32 [4, 192, 3072], P(None, 'gx', 'gy'), may hold values from 0.01 to 0.1
- nest_anchor: int32 [2], replicated, may hold values from 1 to 1791, as said below
Outputs:
- parent_result: float32 [5, 4, 192, 3072], P(None, None, 'gx', 'gy')
- nest_result: float32 [5, 4, 192, 3072], P(None, None, 'gx', 'gy')
Inputs may be any that keep to these rules, and one draw needn't show every extreme that they name: `nest_anchor`: the row anchor is 1 to 126; the column anchor is 1537 to 1791, so the nest with a rim of one parent cell lies inside the parent grid.
All inputs are finite; a program needn't handle non-finite values.
Results may differ from a plain program's by a relative error of at most 0.00002.
Values sent between devices are 32-bit elements; how exact they have to be, the bound alone decides.
No kernel may reach another device: no remote copies, remote signals or barrier semaphores. Data moves between devices by JAX's collectives and lax.ppermute only.
A program may use at most 192 MiB of HBM per device.

v0:
```python
import jax
import jax.numpy as jnp
from jax import lax
from jax.sharding import PartitionSpec as P

SUBSTEPS = 3


third = 1.0 / 3.0
two_thirds = 2.0 / 3.0
nudge_floor = 0.1
relax_width = 4.0


def extended(cells, sides, width):
    for axis, dim in sides:
        count = lax.axis_size(axis)
        ends = count - 1
        head = lax.slice_in_dim(cells, 0, width, axis=dim)
        tail = lax.slice_in_dim(cells, cells.shape[dim] - width, cells.shape[dim], axis=dim)
        cells = jnp.concatenate(
            [
                lax.ppermute(tail, axis, [(i, (i + 1) % count) for i in range(ends)]),
                cells,
                lax.ppermute(head, axis, [((i + 1) % count, i) for i in range(ends)]),
            ],
            axis=dim,
        )
    return cells


def update(values, padded, velocity, mixing):
    western = padded[:, :, :-2, 1:-1]
    eastern = padded[:, :, 2:, 1:-1]
    southern = padded[:, :, 1:-1, :-2]
    northern = padded[:, :, 1:-1, 2:]
    along_rows = velocity[0]
    along_columns = velocity[1]
    upwind = (
        jnp.maximum(along_rows, 0.0) * (values - western)
        + jnp.minimum(along_rows, 0.0) * (eastern - values)
        + jnp.maximum(along_columns, 0.0) * (values - southern)
        + jnp.minimum(along_columns, 0.0) * (northern - values)
    )
    return values - upwind + mixing * (eastern + western + northern + southern - 4.0 * values)


def refine_rows(block):
    lower = block[:, :, :-2]
    centre = block[:, :, 1:-1]
    upper = block[:, :, 2:]
    stacked = jnp.stack(
        (third * lower + two_thirds * centre, centre, two_thirds * centre + third * upper), axis=3
    )
    extent = centre.shape
    return stacked.reshape(extent[0], extent[1], 3 * extent[2], extent[3])


def refine_columns(block):
    lower = block[:, :, :, :-2]
    centre = block[:, :, :, 1:-1]
    upper = block[:, :, :, 2:]
    stacked = jnp.stack(
        (third * lower + two_thirds * centre, centre, two_thirds * centre + third * upper), axis=4
    )
    extent = centre.shape
    return stacked.reshape(extent[0], extent[1], extent[2], 3 * extent[3])


def block_mean(state):
    extent = state.shape
    grouped = state.reshape(extent[0], extent[1], extent[2] // 3, 3, extent[3] // 3, 3)
    return jnp.sum(grouped, axis=(3, 5)) / 9.0


def relax_weight(row_global, column_global, total_rows, total_columns):
    row_distance = jnp.minimum(row_global, total_rows - 1 - row_global)
    column_distance = jnp.minimum(column_global, total_columns - 1 - column_global)
    distance = jnp.minimum(row_distance[:, None], column_distance[None, :]).astype(jnp.float32)
    return nudge_floor + (1.0 - nudge_floor) * jnp.exp(-distance / relax_width)


def take_rows(values, positions, valid):
    picked = jnp.take(values, jnp.clip(positions, 0, values.shape[2] - 1), axis=2)
    return jnp.where(valid[:, None], picked, 0.0)


def take_columns(values, positions, valid):
    picked = jnp.take(values, jnp.clip(positions, 0, values.shape[3] - 1), axis=3)
    return jnp.where(valid, picked, 0.0)


def within(positions, limit):
    return (positions >= 0) & (positions < limit)


def spans(anchor, count, length):
    offsets = (
        jnp.arange(count, dtype=jnp.int32)[:, None] * length
        + jnp.arange(length + 2, dtype=jnp.int32)[None, :]
    )
    return anchor - 1 + offsets.reshape(-1)


def owner_mask(owners, count):
    return (owners[None, :] == jnp.arange(count, dtype=jnp.int32)[:, None]).reshape(-1)


def spread_rows(values, owners, count):
    tiled = jnp.tile(values, (1, 1, count, 1))
    return jnp.where(owner_mask(owners, count)[:, None], tiled, 0.0)


def spread_columns(values, owners, count):
    tiled = jnp.tile(values, (1, 1, 1, count))
    return jnp.where(owner_mask(owners, count), tiled, 0.0)


def per_device(
    parent_fields,
    parent_velocity,
    parent_mixing,
    nest_fields,
    nest_velocity,
    nest_mixing,
    nest_anchor,
):
    row_rank = lax.axis_index("gx")
    column_rank = lax.axis_index("gy")
    row_devices = lax.axis_size("gx")
    column_devices = lax.axis_size("gy")
    fields_count = parent_fields.shape[0]
    levels_count = parent_fields.shape[1]
    parent_rows = parent_fields.shape[2]
    parent_columns = parent_fields.shape[3]
    nest_rows = nest_fields.shape[2]
    nest_columns = nest_fields.shape[3]
    span_rows = nest_rows // 3
    span_columns = nest_columns // 3
    row_anchor = nest_anchor[0]
    column_anchor = nest_anchor[1]
    parent_padded = extended(parent_fields, (("gx", 2), ("gy", 3)), 1)
    parent_next = update(parent_fields, parent_padded, parent_velocity, parent_mixing)
    row_targets = spans(row_anchor, row_devices, span_rows) - row_rank * parent_rows
    column_targets = (
        spans(column_anchor, column_devices, span_columns) - column_rank * parent_columns
    )
    outgoing = take_columns(parent_next, column_targets, within(column_targets, parent_columns))
    incoming = lax.all_to_all(outgoing, "gy", split_axis=3, concat_axis=3, tiled=True)
    partial_block = incoming.reshape(
        fields_count, levels_count, parent_rows, column_devices, span_columns + 2
    ).sum(axis=3)
    outgoing_rows = take_rows(partial_block, row_targets, within(row_targets, parent_rows))
    incoming_rows = lax.all_to_all(outgoing_rows, "gx", split_axis=2, concat_axis=2, tiled=True)
    relay = incoming_rows.reshape(
        fields_count, levels_count, row_devices, span_rows + 2, span_columns + 2
    ).sum(axis=2)
    forcing = refine_columns(refine_rows(relay))
    row_global = row_rank * nest_rows + jnp.arange(nest_rows, dtype=jnp.int32)
    column_global = column_rank * nest_columns + jnp.arange(nest_columns, dtype=jnp.int32)
    weight = relax_weight(
        row_global, column_global, row_devices * nest_rows, column_devices * nest_columns
    )
    state = nest_fields
    for substep in range(SUBSTEPS):
        nest_padded = extended(state, (("gx", 2), ("gy", 3)), 1)
        moved = update(state, nest_padded, nest_velocity, nest_mixing)
        state = moved + weight * (forcing - moved)
    coarse = block_mean(state)
    own_rows = row_anchor + row_rank * span_rows + jnp.arange(span_rows, dtype=jnp.int32)
    own_columns = (
        column_anchor + column_rank * span_columns + jnp.arange(span_columns, dtype=jnp.int32)
    )
    relative_rows = row_rank * parent_rows + jnp.arange(parent_rows, dtype=jnp.int32) - row_anchor
    relative_columns = (
        column_rank * parent_columns + jnp.arange(parent_columns, dtype=jnp.int32) - column_anchor
    )
    rows_valid = within(relative_rows, row_devices * span_rows)
    columns_valid = within(relative_columns, column_devices * span_columns)
    outgoing = spread_columns(coarse, own_columns // parent_columns, column_devices)
    incoming = lax.all_to_all(outgoing, "gy", split_axis=3, concat_axis=3, tiled=True)
    placed = take_columns(incoming, relative_columns, columns_valid)
    outgoing_rows = spread_rows(placed, own_rows // parent_rows, row_devices)
    incoming_rows = lax.all_to_all(outgoing_rows, "gx", split_axis=2, concat_axis=2, tiled=True)
    fed_back = take_rows(incoming_rows, relative_rows, rows_valid)
    covered = rows_valid[:, None] & columns_valid[None, :]
    parent_result = jnp.where(covered, fed_back, parent_next)
    return (parent_result, state)


def solution(mesh):
    placed = (
        P(None, None, "gx", "gy"),
        P(None, None, "gx", "gy"),
        P(None, "gx", "gy"),
        P(None, None, "gx", "gy"),
        P(None, None, "gx", "gy"),
        P(None, "gx", "gy"),
        P(),
    )
    return jax.shard_map(
        per_device,
        mesh=mesh,
        in_specs=placed,
        out_specs=(P(None, None, "gx", "gy"), P(None, None, "gx", "gy")),
        check_vma=False,
    )
```

profile of v0, /device:TPU:1, one launch (start us, length us, event | category | flops | bytes accessed | tf_op | source)
XLA Modules:
  0.0 546.9 jit_solution(9306664756793934417)
XLA Ops:
  29.5 19.9 %gather_fusion = f32[1040,5,4,48]{3,2,1,0:T(4,128)} fusion(f32[5,4,48,384]{2,1,3,0:T(4,128)} %copy.257, s32[2048]{0:T(1024)} %pad_clamp_fusion), kind=kCustom, calls=%fused_computation | custom fusion | bytes 7991360 | tf_op jit(solution)/shard_map/jit(_take)/gather | solution.py:89
  49.3 9.6 %fusion.88 = f32[1040,5,4,48]{3,2,1,0:T(4,128)} fusion(f32[1040,5,4,48]{3,2,1,0:T(4,128)} %gather_fusion, pred[1040]{0:T(1024)(128)(4,1)S(1)} %copy-done.11, pred[1040]{0:T(1024)(128)(4,1)S(1)} %copy-done.12), kind=kLoop, calls=%fused_computation.196 | loop fusion | flops 1996800 | bytes 7989280
  58.9 14.0 %reshape.359 = f32[8,1,124800]{2,1,0:T(1,128)} reshape(f32[1040,5,4,48]{3,2,1,0:T(4,128)} %fusion.88) | data formatting | bytes 7987200
  72.9 5.5 %all-to-all-start = ((f32[8,1,124800]{2,1,0:T(1,128)}), f32[8,1,124800]{2,1,0:T(1,128)}, u32[]{:S(2)}, u32[]{:S(2)}) async-start(f32[8,1,124800]{2,1,0:T(1,128)} %reshape.359), calls=%async_computation | async-start | bytes 7987200 | tf_op jit(solution)/shard_map/all_to_all | solution.py:149
  79.1 5.3 collective-permute-start
  98.7 69.0 %all-to-all-done = f32[8,1,124800]{2,1,0:T(1,128)} async-done(((f32[8,1,124800]{2,1,0:T(1,128)}), f32[8,1,124800]{2,1,0:T(1,128)}, u32[]{:S(2)}, u32[]{:S(2)}) %all-to-all-start) | async-done | bytes 3993632 | tf_op jit(solution)/shard_map/all_to_all | solution.py:149
  168.3 13.2 %reduce.4 = f32[8,124800]{1,0:T(8,128)} reduce(f32[8,1,124800]{2,1,0:T(1,128)} %all-to-all-done, f32[]{:T(128)} %broadcast.601), dimensions={1}, to_apply=%all_to_all.12.reduce_sub_computation | reduce | bytes 7987204 | tf_op jit(solution)/shard_map/all_to_all | solution.py:149
  181.5 14.5 %reshape.360 = f32[1040,5,4,48]{3,2,1,0:T(4,128)} reshape(f32[8,124800]{1,0:T(8,128)} %reduce.4) | data formatting | bytes 7987200
  196.0 7.7 %reduce_sum.27 = f32[5,4,48,130]{2,1,0,3:T(4,128)} reduce(f32[5,4,48,8,130]{2,1,0,4,3:T(4,128)} %bitcast.61, f32[]{:T(128)} %constant.66.clone.1), dimensions={3}, to_apply=%region_0.1 | reduce | flops 873600 | bytes 4492804 | tf_op jit(solution)/shard_map/reduce_sum | solution.py:152
  203.7 13.9 %copy.258 = f32[5,4,48,130]{3,1,2,0:T(4,128)} copy(f32[5,4,48,130]{2,1,0,3:T(4,128)} %reduce_sum.27) | data formatting | bytes 998400 | tf_op jit(solution)/shard_map/reduce_sum | solution.py:152
  258.2 5.9 %multiply_add_fusion.2 = f32[5,4,48,384]{3,2,1,0:T(8,128)S(1)} fusion(f32[5,4,48,384]{3,2,1,0:T(8,128)S(1)} %copy.263, f32[5,4,48,384]{3,2,1,0:T(8,128)} %param.10, f32[5,4,50,1]{3,2,1,0:T(8,128)} %copy.246, f32[5,4,1,384]{3,2,1,0:T(1,128)} %copy-done.6, f32[5,4,1,384]{3,2,1,0:T(1,128)} %copy-done.5, f32[5,4,50,1]{3,2,1,0:T(8,128)} %copy.244, ...), kind=kLoop, calls=%fused_computation.103 | loop fusion | flops 11059200 | bytes 6041408 | tf_op jit(solution)/shard_map/add | solution.py:168
  287.5 5.4 multiply_add_fusion.1
  315.9 6.3 %multiply_add_fusion = f32[5,4,48,384]{3,2,1,0:T(8,128)} fusion(f32[5,4,48,384]{3,2,1,0:T(8,128)S(1)} %copy.263, f32[5,4,48,384]{3,2,1,0:T(8,128)} %copy-done.1, f32[5,4,50,1]{3,2,1,0:T(8,128)} %copy.284, f32[5,4,1,384]{3,2,1,0:T(1,128)} %copy-done.9, f32[5,4,1,384]{3,2,1,0:T(1,128)} %copy-done.7, f32[5,4,50,1]{3,2,1,0:T(8,128)} %copy.282, ...), kind=kLoop, calls=%fused_computation.101 | loop fusion | flops 11059200 | bytes 6041408 | tf_op jit(solution)/shard_map/add | solution.py:168
  322.2 61.7 %reshape.322 = f32[5,4,16,3,128,3]{5,4,3,2,1,0:T(8,128)} reshape(f32[5,4,48,384]{3,2,1,0:T(8,128)} %multiply_add_fusion) | data formatting | bytes 2949120 | tf_op jit(solution)/shard_map/reshape | solution.py:72
  383.9 20.5 %reduce_sum.29 = f32[5,4,16,128]{3,2,1,0:T(8,128)S(1)} reduce(f32[5,4,16,3,128,3]{5,4,3,2,1,0:T(8,128)} %reshape.322, f32[]{:T(128)} %constant.66.clone.1), dimensions={3,5}, to_apply=%region_2.3 | reduce | flops 327680 | bytes 1638404 | tf_op jit(solution)/shard_map/reduce_sum | solution.py:73
  404.9 6.7 %bitcast_select_fusion = f32[5,4,16,1024]{2,1,0,3:T(4,128)} fusion(f32[5,4,16,128]{2,1,0,3:T(4,128)S(1)} %copy.286, pred[1024]{0:T(1024)(128)(4,1)} %fusion.70), kind=kLoop, calls=%fused_computation.5 | loop fusion | flops 327680 | bytes 1475584 | tf_op jit(solution)/shard_map/jit(_where)/select_n | solution.py:116
  411.6 11.4 %reshape.361 = f32[8,1,40960]{2,1,0:T(1,128)} reshape(f32[1024,5,4,16]{3,2,1,0:T(4,128)} %bitcast.62) | data formatting | bytes 2621440
  430.3 28.7 %all-to-all-done.2 = f32[8,1,40960]{2,1,0:T(1,128)S(1)} async-done(((f32[8,1,40960]{2,1,0:T(1,128)}), f32[8,1,40960]{2,1,0:T(1,128)S(1)}, u32[]{:S(2)}, u32[]{:S(2)}) %all-to-all-start.2) | async-done | bytes 1310752 | tf_op jit(solution)/shard_map/all_to_all | solution.py:181
  459.1 5.2 reduce.5
  464.3 12.5 %reshape.362 = f32[1024,5,4,16]{3,2,1,0:T(4,128)} reshape(f32[8,40960]{1,0:T(8,128)} %reduce.5) | data formatting | bytes 2621440
  476.8 9.8 %copy.287 = f32[5,4,16,1024]{2,1,3,0:T(4,128)} copy(f32[5,4,16,1024]{2,1,0,3:T(4,128)} %bitcast.63) | data formatting | bytes 2621440 | tf_op jit(solution)/shard_map/all_to_all | solution.py:181
  486.5 9.7 %gather_fusion.2 = f32[384,5,4,16]{3,2,1,0:T(4,128)} fusion(f32[5,4,16,1024]{2,1,3,0:T(4,128)} %copy.287, s32[1024]{0:T(1024)S(1)} %pad_clamp_fusion.2), kind=kCustom, calls=%fused_computation.2 | custom fusion | bytes 984576 | tf_op jit(solution)/shard_map/jit(_take)/gather | solution.py:89
  496.2 5.9 %select_bitcast_fusion.1 = f32[5,4,16,384]{2,1,0,3:T(4,128)} fusion(f32[384,5,4,16]{3,2,1,0:T(4,128)} %gather_fusion.2, pred[384]{0:T(512)(128)(4,1)S(1)} %fusion.77, pred[384]{0:T(512)(128)(4,1)S(1)} %compare_and_fusion.2), kind=kLoop, calls=%fused_computation.6 | loop fusion | flops 245760 | bytes 983808 | tf_op jit(solution)/shard_map/jit(_where)/select_n | solution.py:90
  514.9 20.6 %all-to-all-done.3 = f32[5,4,64,384]{3,1,0,2:T(4,128)} async-done(((f32[5,4,64,384]{3,1,0,2:T(4,128)}), f32[5,4,64,384]{3,1,0,2:T(4,128)}, u32[]{:S(2)}, u32[]{:S(2)}) %all-to-all-start.3) | async-done | bytes 1966112 | tf_op jit(solution)/shard_map/all_to_all | solution.py:184
  (162 shorter events, 160.2 us)
Async XLA Ops:
  0.6 12.9 %copy-start = (f32[5,4,48,384]{3,2,1,0:T(8,128)S(1)}, f32[5,4,48,384]{3,2,1,0:T(8,128)}, u32[]{:S(2)}) copy-start(f32[5,4,48,384]{3,2,1,0:T(8,128)} %param.7) | copy-start | bytes 4423684
  1.9 11.5 %collective-permute-start.4 = (f32[5,4,1,384]{3,1,2,0:T(4,128)S(1)}, f32[5,4,1,384]{3,1,2,0:T(4,128)S(1)}, u32[]{:S(2)}, u32[]{:S(2)}) collective-permute-start(f32[5,4,1,384]{3,1,2,0:T(4,128)S(1)} %copy.294), channel_id=1, source_target_pairs={{0,8},{8,16},{16,24},{1,9},{9,17},{17,25},{2,10},{10,18},{18,26},{... | collective-permute-start | bytes 92168 | tf_op jit(solution)/shard_map/ppermute | solution.py:23
  6.4 7.0 %collective-permute-start.5 = (f32[5,4,1,384]{3,1,2,0:T(4,128)S(1)}, f32[5,4,1,384]{3,1,2,0:T(4,128)S(1)}, u32[]{:S(2)}, u32[]{:S(2)}) collective-permute-start(f32[5,4,1,384]{3,1,2,0:T(4,128)S(1)} %copy.295), channel_id=1, source_target_pairs={{8,0},{16,8},{24,16},{9,1},{17,9},{25,17},{10,2},{18,10},{26,18},{... | collective-permute-start | bytes 92168 | tf_op jit(solution)/shard_map/ppermute | solution.py:25
  14.1 5.9 %collective-permute-start.6 = (f32[5,4,50,1]{2,1,3,0:T(4,128)S(1)}, f32[5,4,50,1]{2,1,3,0:T(4,128)S(1)}, u32[]{:S(2)}, u32[]{:S(2)}) collective-permute-start(f32[5,4,50,1]{2,1,3,0:T(4,128)S(1)} %copy.253), channel_id=1, source_target_pairs={{0,1},{1,2},{2,3},{3,4},{4,5},{5,6},{6,7},{8,9},{9,10},{10,11},{11... | collective-permute-start | bytes 12008 | tf_op jit(solution)/shard_map/ppermute | solution.py:23
  17.5 4.4 collective-permute-start.7
  29.5 19.9 %copy-start.11 = (pred[1040]{0:T(1024)(128)(4,1)S(1)}, pred[1040]{0:T(1024)(128)(4,1)}, u32[]{:S(2)}) copy-start(pred[1040]{0:T(1024)(128)(4,1)} %compare_and_fusion) | copy-start | bytes 3124
  29.5 19.9 %copy-start.12 = (pred[1040]{0:T(1024)(128)(4,1)S(1)}, pred[1040]{0:T(1024)(128)(4,1)}, u32[]{:S(2)}) copy-start(pred[1040]{0:T(1024)(128)(4,1)} %reshape.324) | copy-start | bytes 3124
  72.9 94.8 %all-to-all-start = ((f32[8,1,124800]{2,1,0:T(1,128)}), f32[8,1,124800]{2,1,0:T(1,128)}, u32[]{:S(2)}, u32[]{:S(2)}) async-start(f32[8,1,124800]{2,1,0:T(1,128)} %reshape.359), calls=%async_computation | async-start | bytes 7987200 | tf_op jit(solution)/shard_map/all_to_all | solution.py:149
  79.1 151.6 %collective-permute-start = (f32[5,4,1,384]{3,1,2,0:T(4,128)}, f32[5,4,1,384]{3,1,2,0:T(4,128)}, u32[]{:S(2)}, u32[]{:S(2)}) collective-permute-start(f32[5,4,1,384]{3,1,2,0:T(4,128)} %copy.292), channel_id=1, source_target_pairs={{0,8},{8,16},{16,24},{1,9},{9,17},{17,25},{2,10},{10,18},{18,26},{... | collective-permute-start | bytes 92168 | tf_op jit(solution)/shard_map/ppermute | solution.py:23
  85.1 146.4 %collective-permute-start.1 = (f32[5,4,1,384]{3,1,2,0:T(4,128)}, f32[5,4,1,384]{3,1,2,0:T(4,128)}, u32[]{:S(2)}, u32[]{:S(2)}) collective-permute-start(f32[5,4,1,384]{3,1,2,0:T(4,128)} %copy.293), channel_id=1, source_target_pairs={{8,0},{16,8},{24,16},{9,1},{17,9},{25,17},{10,2},{18,10},{26,18},{... | collective-permute-start | bytes 92168 | tf_op jit(solution)/shard_map/ppermute | solution.py:25
  224.6 23.2 %all-to-all-start.1 = ((f32[5,4,72,130]{3,1,0,2:T(4,128)}), f32[5,4,72,130]{3,1,0,2:T(4,128)}, u32[]{:S(2)}, u32[]{:S(2)}) async-start(f32[5,4,72,130]{3,1,0,2:T(4,128)} %select_bitcast_fusion.2), calls=%async_computation.1 | async-start | bytes 2949120 | tf_op jit(solution)/shard_map/all_to_all | solution.py:154
  234.9 7.1 %collective-permute-start.2 = (f32[5,4,50,1]{2,1,3,0:T(4,128)S(1)}, f32[5,4,50,1]{2,1,3,0:T(4,128)S(1)}, u32[]{:S(2)}, u32[]{:S(2)}) collective-permute-start(f32[5,4,50,1]{2,1,3,0:T(4,128)S(1)} %copy.243), channel_id=1, source_target_pairs={{0,1},{1,2},{2,3},{3,4},{4,5},{5,6},{6,7},{8,9},{9,10},{10,11},{11... | collective-permute-start | bytes 12008 | tf_op jit(solution)/shard_map/ppermute | solution.py:23
  239.3 4.8 collective-permute-start.3
  264.1 4.7 collective-permute-start.8
  266.9 5.2 collective-permute-start.9
  275.3 7.5 %collective-permute-start.10 = (f32[5,4,50,1]{2,1,3,0:T(4,128)}, f32[5,4,50,1]{2,1,3,0:T(4,128)}, u32[]{:S(2)}, u32[]{:S(2)}) collective-permute-start(f32[5,4,50,1]{2,1,3,0:T(4,128)} %copy.270), channel_id=1, source_target_pairs={{0,1},{1,2},{2,3},{3,4},{4,5},{5,6},{6,7},{8,9},{9,10},{10,11},{11... | collective-permute-start | bytes 12008 | tf_op jit(solution)/shard_map/ppermute | solution.py:23
  280.9 4.7 collective-permute-start.11
  292.9 10.0 %copy-start.1 = (f32[5,4,48,384]{3,2,1,0:T(8,128)}, f32[5,4,48,384]{3,2,1,0:T(8,128)S(1)}, u32[]{:S(2)}) copy-start(f32[5,4,48,384]{3,2,1,0:T(8,128)S(1)} %multiply_add_fusion.1) | copy-start | bytes 4423684
  292.9 5.9 %collective-permute-start.12 = (f32[5,4,1,384]{3,1,2,0:T(4,128)S(1)}, f32[5,4,1,384]{3,1,2,0:T(4,128)S(1)}, u32[]{:S(2)}, u32[]{:S(2)}) collective-permute-start(f32[5,4,1,384]{3,1,2,0:T(4,128)S(1)} %copy.275), channel_id=1, source_target_pairs={{0,8},{8,16},{16,24},{1,9},{9,17},{17,25},{2,10},{10,18},{18,26},{... | collective-permute-start | bytes 92168 | tf_op jit(solution)/shard_map/ppermute | solution.py:23
  296.3 5.2 collective-permute-start.13
  304.7 7.2 %collective-permute-start.14 = (f32[5,4,50,1]{2,1,3,0:T(4,128)}, f32[5,4,50,1]{2,1,3,0:T(4,128)}, u32[]{:S(2)}, u32[]{:S(2)}) collective-permute-start(f32[5,4,50,1]{2,1,3,0:T(4,128)} %copy.281), channel_id=1, source_target_pairs={{0,1},{1,2},{2,3},{3,4},{4,5},{5,6},{6,7},{8,9},{9,10},{10,11},{11... | collective-permute-start | bytes 12008 | tf_op jit(solution)/shard_map/ppermute | solution.py:23
  309.4 4.7 collective-permute-start.15
  423.0 36.0 %all-to-all-start.2 = ((f32[8,1,40960]{2,1,0:T(1,128)}), f32[8,1,40960]{2,1,0:T(1,128)S(1)}, u32[]{:S(2)}, u32[]{:S(2)}) async-start(f32[8,1,40960]{2,1,0:T(1,128)} %reshape.361), calls=%async_computation.2 | async-start | bytes 2621440 | tf_op jit(solution)/shard_map/all_to_all | solution.py:181
  507.3 28.2 %all-to-all-start.3 = ((f32[5,4,64,384]{3,1,0,2:T(4,128)}), f32[5,4,64,384]{3,1,0,2:T(4,128)}, u32[]{:S(2)}, u32[]{:S(2)}) async-start(f32[5,4,64,384]{3,1,0,2:T(4,128)} %bitcast_select_fusion.1), calls=%async_computation.3 | async-start | bytes 3932160 | tf_op jit(solution)/shard_map/all_to_all | solution.py:184
  (11 other events, 28.5 us)
where the time goes:
time: 558 us; the launch traced here: 547 us
  local copies, waits for them, and re-layouts  225 us (40%)
  waiting for transfers between devices  131 us (23%)
  other arithmetic  126 us (23%)
  starting transfers between devices  61.4 us (11%)
    all_to_all x2, waiting for transfers between devices, per_device(): lax.all_to_all(outgoing, 'gy', split_axis=3, concat_axis=3, tiled=True)  97.7 us
    reshape x1, local copies, waits for them, and re-layouts, block_mean(): state.reshape(extent[0], extent[1], extent[2] // 3, 3, extent[3] // 3, 3)  61.7 us
    unnamed x38, local copies, waits for them, and re-layouts  54.3 us
    gather x2, local copies, waits for them, and re-layouts, take_columns(): jnp.take(values, jnp.clip(positions, 0, values.shape[3] - 1), axis=3)  29.5 us
    ppermute x8, starting transfers between devices, extended(): lax.ppermute(tail, axis, [(i, (i + 1) % count) for i in range(ends)])  28.6 us
    all_to_all x2, waiting for transfers between devices, per_device(): lax.all_to_all(outgoing_rows, 'gx', split_axis=2, concat_axis=2, tiled=True)  23.1 us
    reduce_sum x1, other arithmetic, block_mean(): return jnp.sum(grouped, axis=(3, 5)) / 9.0  20.5 us
    all_to_all x2, other arithmetic, per_device(): lax.all_to_all(outgoing, 'gy', split_axis=3, concat_axis=3, tiled=True)  18.4 us
  transfers between devices with their start and end apart: 20, of which 10 were waited for; matrix products, arithmetic and copies ran while one was open for 18% of the time, Pallas kernels for 0%

commit v1 on v0

v1 whole, which is shorter than its diff:
```python
import functools

import jax
import jax.numpy as jnp
import numpy as np
from jax import lax
from jax.experimental import pallas as pl
from jax.experimental.pallas import tpu as pltpu
from jax.sharding import PartitionSpec as P

SUBSTEPS = 3
F32 = jnp.float32
LANES = 128
VMEM_LIMIT = 56 * 1024 * 1024
nudge_floor = 0.1
relax_width = 4.0


def call(body, outs, ins, smem=0, scratch=()):
    specs = [pl.BlockSpec(memory_space=pltpu.SMEM)] * smem + [
        pl.BlockSpec(memory_space=pltpu.VMEM)
    ] * (len(ins) - smem)
    return pl.pallas_call(
        body,
        out_shape=[jax.ShapeDtypeStruct(shape, F32) for shape in outs],
        in_specs=specs,
        out_specs=[pl.BlockSpec(memory_space=pltpu.VMEM)] * len(outs),
        scratch_shapes=list(scratch),
        compiler_params=pltpu.CompilerParams(vmem_limit_bytes=VMEM_LIMIT),
    )(*ins)


def lane_index(rows, lanes=LANES):
    return lax.broadcasted_iota(jnp.int32, (rows, lanes), 1)


def row_index(rows, lanes=LANES):
    return lax.broadcasted_iota(jnp.int32, (rows, lanes), 0)


def halo_exchange(axis, to_next, to_previous):
    ends = lax.axis_size(axis) - 1
    from_previous = lax.ppermute(to_next, axis, [(i, i + 1) for i in range(ends)])
    from_next = lax.ppermute(to_previous, axis, [(i + 1, i) for i in range(ends)])
    return from_previous, from_next


def pack_kernel(pf, nf, nv, nm, rows_next, rows_prev, cols_next, cols_prev):
    channels, rows, columns = pf.shape
    coefs = nv.shape[0] + nm.shape[0]
    for ch in range(channels):
        for at in range(3):
            here = at * channels + ch
            rows_next[here : here + 1, :] = nf[ch, rows - 3 + at : rows - 2 + at, :]
            rows_prev[here : here + 1, :] = nf[ch, at : at + 1, :]
    base = 3 * channels
    for cc in range(coefs):
        ref, row = (nv, cc) if cc < nv.shape[0] else (nm, cc - nv.shape[0])
        for at in range(2):
            here = base + at * coefs + cc
            rows_next[here : here + 1, :] = ref[row, rows - 2 + at : rows - 1 + at, :]
            rows_prev[here : here + 1, :] = ref[row, at : at + 1, :]
    base = base + 2 * coefs
    for ch in range(channels):
        rows_next[base + ch : base + ch + 1, :] = pf[ch, rows - 1 : rows, :]
        rows_prev[base + ch : base + ch + 1, :] = pf[ch, 0:1, :]
    lanes = lane_index(rows)
    last = jnp.zeros((rows, LANES), F32)
    first = jnp.zeros((rows, LANES), F32)
    for ch in range(channels):
        tail = pltpu.roll(pf[ch, :, columns - LANES :], (ch + 1) % LANES, 1)
        head = pltpu.roll(pf[ch, :, :LANES], ch, 1)
        last = jnp.where(lanes == ch, tail, last)
        first = jnp.where(lanes == ch, head, first)
    cols_next[...] = last
    cols_prev[...] = first


def parent_kernel(anchor, pf, pv, pm, top, bottom, left, right, *rest):
    parent_next, slabs = rest[0], rest[1:]
    channels, rows, columns = pf.shape
    levels = pm.shape[0]
    span = rows // 3
    rank, size_x = lax.axis_index("gx"), lax.axis_size("gx")
    half = lax.axis_size("gy") // 2 * columns
    base = 3 * channels + 2 * 3 * levels
    offset = anchor[1] - half
    shift = lax.rem(2 * columns - offset, columns)
    row_shift = lax.rem((rows - span) * rank + size_x * rows - anchor[0], rows)
    row = row_index(rows, columns)
    column = lane_index(rows, columns)

    def level_body(level, carry):
        u = pv[level]
        v = pv[levels + level]
        k = pm[level]
        a_w = jnp.maximum(u, 0.0) + k
        a_e = k - jnp.minimum(u, 0.0)
        a_s = jnp.maximum(v, 0.0) + k
        a_n = k - jnp.minimum(v, 0.0)
        a_c = 1.0 - (a_w + a_e + a_s + a_n)
        def field_body(field, carry):
            ch = field * levels + level
            q = pf[ch]
            west = jnp.where(row == 0, top[pl.ds(base + ch, 1), :], pltpu.roll(q, 1, 0))
            east = jnp.where(
                row == rows - 1, bottom[pl.ds(base + ch, 1), :], pltpu.roll(q, rows - 1, 0)
            )
            pad = jnp.zeros((rows, columns - LANES), F32)
            at_first = pltpu.roll(left[...], LANES - ch, 1)
            at_last = pltpu.roll(right[...], LANES - 1 - ch, 1)
            south = jnp.where(
                column == 0, jnp.concatenate([at_first, pad], axis=1), pltpu.roll(q, 1, 1)
            )
            north = jnp.where(
                column == columns - 1,
                jnp.concatenate([pad, at_last], axis=1),
                pltpu.roll(q, columns - 1, 1),
            )
            result = a_c * q + a_w * west + a_e * east + a_s * south + a_n * north
            parent_next[ch] = result
            moved = pltpu.roll(pltpu.roll(result, shift, 1), row_shift, 0)
            for tile, slab in enumerate(slabs):
                first = span * tile
                slab[pl.ds(pl.multiple_of(span * ch, 8), span), :] = moved[first : first + span]
                before, after = (first - 1) % rows, (first + span) % rows
                slab[pl.ds(span * channels + ch, 1), :] = moved[before : before + 1]
                slab[pl.ds((span + 1) * channels + ch, 1), :] = moved[after : after + 1]
            return carry

        return lax.fori_loop(0, pf.shape[0] // levels, field_body, carry)

    lax.fori_loop(0, levels, level_body, 0)


def pick(index, choices):
    value = choices[0][1]
    for key, other in choices[1:]:
        value = jnp.where(index == key, other, value)
    return value


def row_select_kernel(shifts, rows, anchor, *refs):
    count = len(shifts)
    slabs, messages = refs[:count], refs[count:]
    span = rows // 3
    total, columns = slabs[0].shape
    channels = total // (span + 2)
    rank = lax.axis_index("gx")
    start = anchor[0] + span * rank
    lowest, highest = lax.div(start, rows), lax.div(start + span - 1, rows)
    above, below = lax.div(start - 1, rows), lax.div(start + span, rows)
    split = jnp.where(highest > lowest, rows * highest - start, span)
    row = row_index(span)
    lanes, rim_lanes = lane_index(span), lane_index(1)

    def views(first, size, tile):
        return [
            (d, ref[first : first + size, LANES * tile : LANES * (tile + 1)])
            for d, ref in zip(shifts, slabs)
        ]

    def edges(rims, tiles, mask, ch):
        for tile in range(3):
            before = pltpu.roll(tiles[(tile + 2) % 3], (2 * ch + 1) % LANES, 1)
            after = pltpu.roll(tiles[(tile + 1) % 3], 2 * ch + 1, 1)
            rim = jnp.where(mask == 2 * ch, before, rims[tile])
            rims[tile] = jnp.where(mask == 2 * ch + 1, after, rim)

    rims = [jnp.zeros((span, LANES), F32) for _ in range(3)]
    for ch in range(channels):
        tiles = []
        for tile in range(3):
            choices = views(span * ch, span, tile)
            low, high = pick(rank - lowest, choices), pick(rank - highest, choices)
            value = jnp.where(row < split, low, high)
            messages[tile][span * ch : span * (ch + 1), :] = value
            tiles.append(value)
        edges(rims, tiles, lanes, ch)
    for side, owner in enumerate((above, below)):
        first = (span + side) * channels
        tiles = [pick(rank - owner, views(first, channels, tile)) for tile in range(3)]
        side_rims = [jnp.zeros((1, LANES), F32) for _ in range(3)]
        for ch in range(channels):
            edges(side_rims, [value[ch : ch + 1] for value in tiles], rim_lanes, ch)
        for tile in range(3):
            messages[tile][first : first + channels, :] = tiles[tile]
            messages[tile][total + span + side : total + span + side + 1, :] = side_rims[tile]
    for tile in range(3):
        messages[tile][total : total + span, :] = rims[tile]
        padding = messages[tile].shape[0] - total - span - 2
        messages[tile][total + span + 2 :, :] = jnp.zeros((padding, LANES), F32)


def nest_columns_kernel(nf, nv, nm, top, bottom, cols_next, cols_prev, block):
    channels, rows, columns = nf.shape
    height = rows + 8
    lanes = lane_index(height)
    coefs = nv.shape[0] + nm.shape[0]
    block[...] = jnp.zeros_like(block)

    def halo(target, ref, source, first_lane):
        block[target : target + 1, :] = ref[source : source + 1, first_lane : first_lane + LANES]

    def packed(first_lane, moved):
        accumulated = jnp.zeros((height, LANES), F32)
        for ch in range(channels):
            block[0:rows, :] = nf[ch, :, first_lane : first_lane + LANES]
            for at in range(3):
                here = at * channels + ch
                halo(rows + at, bottom, here, first_lane)
                halo(height - 3 + at, top, here, first_lane)
            shift = 3 * ch + (3 if moved else 0)
            inside = (lanes >= 3 * ch) & (lanes < 3 * ch + 3)
            accumulated = jnp.where(inside, pltpu.roll(block[...], shift, 1), accumulated)
        base = 3 * channels
        for cc in range(coefs):
            ref, row = (nv, cc) if cc < nv.shape[0] else (nm, cc - nv.shape[0])
            here = base + 2 * cc
            block[0:rows, :] = ref[row, :, first_lane : first_lane + LANES]
            for at in range(2):
                source = base + at * coefs + cc
                halo(rows + at, bottom, source, first_lane)
                halo(height - 2 + at, top, source, first_lane)
            shift = (here + (2 if moved else 0)) % LANES
            inside = (lanes >= here) & (lanes < here + 2)
            accumulated = jnp.where(inside, pltpu.roll(block[...], shift, 1), accumulated)
        return accumulated

    cols_next[...] = packed(columns - LANES, True)
    cols_prev[...] = packed(0, False)


def three_parts(x):
    high = x.astype(jnp.bfloat16)
    rest = x - high.astype(F32)
    middle = rest.astype(jnp.bfloat16)
    low = (rest - middle.astype(F32)).astype(jnp.bfloat16)
    return high, middle, low


def exact_dot(x, matrix):
    parts = three_parts(x)
    total = jnp.dot(parts[2], matrix, preferred_element_type=F32)
    total = total + jnp.dot(parts[1], matrix, preferred_element_type=F32)
    return total + jnp.dot(parts[0], matrix, preferred_element_type=F32)


def nest_kernel(
    ks, anchor, spread, gather, nf, nv, nm, top, bottom, left, right, *refs
):
    count = len(ks)
    received = dict(zip(ks, refs[:count]))
    result, coarse = refs[count : count + 2]
    relay, refined, forcing, weights, coefs, state, sums, final = refs[count + 2 :]
    channels, rows, columns = nf.shape
    levels = nm.shape[0]
    span_rows, span_columns = rows // 3, columns // 3
    height, width = rows + 8, columns + LANES
    tiles = width // LANES
    relay_rows = span_rows + 2
    total = relay_rows * channels
    rank_x, rank_y = lax.axis_index("gx"), lax.axis_index("gy")
    offset = anchor[1] - lax.axis_size("gy") // 2 * columns
    kind = lax.rem(rank_y, 3)
    edge = columns - offset - span_columns * kind

    lower = pick(kind, [(0, received[0][...]), (1, received[1][...]), (2, received[2][...])])
    upper = jnp.where(kind == 1, received[-2][...], received[-1][...])
    lanes = lane_index(lower.shape[0])
    relay[:, 0:LANES] = jnp.where(lanes < edge, lower, upper)
    relay[:, LANES:] = jnp.zeros((relay.shape[0], LANES), F32)
    rim_low, rim_high = lower[total : total + relay_rows], upper[total : total + relay_rows]
    odd = (lane_index(relay_rows) & 1) == 1
    rim = jnp.where(jnp.where(odd, LANES, -1) < edge, rim_low, rim_high)
    for ch in range(channels):
        sides = pltpu.roll(rim, (LANES - 2 * ch) % LANES, 1)
        relay[span_rows * ch : span_rows * (ch + 1), LANES:] = sides[0:span_rows]
        for side in (span_rows, span_rows + 1):
            here = side * channels + ch
            relay[here : here + 1, LANES:] = sides[side : side + 1]
    refined[...] = exact_dot(relay[...], spread[...])

    row = row_index(height, width)
    column = lane_index(height, width)
    local_row = jnp.where(row < rows + 4, row, row - height)
    local_column = jnp.where(column < columns + LANES // 2, column, column - width)
    global_row = rank_x * rows + local_row
    global_column = rank_y * columns + local_column
    row_distance = jnp.minimum(global_row, lax.axis_size("gx") * rows - 1 - global_row)
    column_distance = jnp.minimum(
        global_column, lax.axis_size("gy") * columns - 1 - global_column
    )
    distance = jnp.minimum(row_distance, column_distance)
    weight = nudge_floor + (1.0 - nudge_floor) * jnp.exp(
        jnp.maximum(distance, 0).astype(F32) / -relax_width
    )
    weight = jnp.where(distance < 0, 0.0, weight)
    weights[...] = weight / 9.0
    keep = 1.0 - weight
    state[...] = jnp.zeros_like(state)
    forcing[...] = jnp.zeros_like(forcing)
    edge_lanes = lane_index(height)
    relay_row = row_index(span_rows, width)

    def side_tile(first, size):
        after = pltpu.roll(right[...], lax.rem(2 * LANES - first, LANES), 1)
        before = pltpu.roll(left[...], lax.rem(2 * LANES - first - size, LANES), 1)
        inside = jnp.where(edge_lanes < LANES // 2, after, before)
        outside = (edge_lanes >= size) & (edge_lanes < LANES - size)
        return jnp.where(outside, 0.0, inside)

    def coef_field(slot, cc, ref, at):
        base = 3 * channels + cc
        coefs[slot, 0:rows, 0:columns] = ref[at]
        for step in range(2):
            source = pl.ds(base + 3 * levels * step, 1)
            coefs[slot, rows + step : rows + step + 1, 0:columns] = bottom[source, :]
            target = height - 2 + step
            coefs[slot, target : target + 1, 0:columns] = top[source, :]
        coefs[slot, :, columns:width] = side_tile(3 * channels + 2 * cc, 2)
        return coefs[slot]

    coefs[:, rows : rows + 8, :] = jnp.zeros((5, 8, width), F32)

    def level_body(level, carry):
        u = coef_field(0, level, nv, level)
        v = coef_field(1, levels + level, nv, levels + level)
        k = coef_field(2, 2 * levels + level, nm, level)
        a_w = jnp.maximum(u, 0.0) + k
        a_e = k - jnp.minimum(u, 0.0)
        a_s = jnp.maximum(v, 0.0) + k
        a_n = k - jnp.minimum(v, 0.0)
        a_c = 1.0 - (a_w + a_e + a_s + a_n)
        coefs[0] = keep * a_c
        coefs[1] = keep * a_w
        coefs[2] = keep * a_e
        coefs[3] = keep * a_s
        coefs[4] = keep * a_n

        def field_body(field, carry):
            ch = field * levels + level
            centre = refined[pl.ds(pl.multiple_of(span_rows * ch, 8), span_rows), :]
            above = refined[pl.ds(span_rows * channels + ch, 1), :]
            below = refined[pl.ds((span_rows + 1) * channels + ch, 1), :]
            before = jnp.where(relay_row == 0, above, pltpu.roll(centre, 1, 0))
            after = jnp.where(
                relay_row == span_rows - 1, below, pltpu.roll(centre, span_rows - 1, 0)
            )
            thirds = (before + 2.0 * centre, 3.0 * centre, 2.0 * centre + after)
            rims = (
                (rows, centre[span_rows - 1 :] + 2.0 * below),
                (rows + 1, 3.0 * below),
                (height - 2, 3.0 * above),
                (height - 1, 2.0 * above + centre[0:1]),
            )
            pulls = []
            for tile in range(tiles):
                part = slice(LANES * tile, LANES * (tile + 1))
                for at, value in enumerate(thirds):
                    forcing[tile, pl.ds(at, span_rows, stride=3), :] = value[:, part]
                for at, value in rims:
                    forcing[tile, at : at + 1, :] = value[:, part]
                pulls.append(weights[:, part] * forcing[tile])
            pull = jnp.concatenate(pulls, axis=1)
            state[0:rows, 0:columns] = nf[ch]
            for step in range(3):
                source = pl.ds(channels * step + ch, 1)
                state[rows + step : rows + step + 1, 0:columns] = bottom[source, :]
                target = height - 3 + step
                state[target : target + 1, 0:columns] = top[source, :]
            state[:, columns:width] = side_tile(3 * ch, 3)
            for _ in range(SUBSTEPS):
                q = state[...]
                state[...] = (
                    pull
                    + coefs[0] * q
                    + coefs[1] * pltpu.roll(q, 1, 0)
                    + coefs[2] * pltpu.roll(q, height - 1, 0)
                    + coefs[3] * pltpu.roll(q, 1, 1)
                    + coefs[4] * pltpu.roll(q, width - 1, 1)
                )
            result[ch] = state[0:rows, 0:columns]
            for tile in range(tiles - 1):
                part = slice(LANES * tile, LANES * (tile + 1))
                final[tile] = state[0:rows, part]
                sums[pl.ds(pl.multiple_of(span_rows * ch, 8), span_rows), part] = (
                    final[tile, pl.ds(0, span_rows, stride=3), :]
                    + final[tile, pl.ds(1, span_rows, stride=3), :]
                    + final[tile, pl.ds(2, span_rows, stride=3), :]
                )
            return carry

        return lax.fori_loop(0, channels // levels, field_body, carry)

    lax.fori_loop(0, levels, level_body, 0)
    coarse[...] = exact_dot(sums[...], gather[...]) / 9.0


def column_select_kernel(ks, columns, anchor, *refs):
    received = dict(zip(ks, refs[: len(ks)]))
    placed = refs[-1]
    offset = anchor[1] - lax.axis_size("gy") // 2 * columns
    lanes = lane_index(placed.shape[0])
    placed[:, 0:LANES] = received[0][...]
    for tile in (1, 2):
        own = lanes < columns - offset - LANES * tile
        placed[:, LANES * tile : LANES * (tile + 1)] = jnp.where(
            own, received[tile][...], received[tile - 3][...]
        )


def merge_kernel(shifts, anchor, parent_next, *refs):
    slabs = refs[: len(shifts)]
    merged = refs[len(shifts)]
    channels, rows, columns = parent_next.shape
    span = rows // 3
    rank_x, rank_y = lax.axis_index("gx"), lax.axis_index("gy")
    size_x, size_y = lax.axis_size("gx"), lax.axis_size("gy")
    offset = anchor[1] - size_y // 2 * columns
    shift = lax.rem(offset + columns, columns)
    row = rank_x * rows + row_index(rows, columns) - anchor[0]
    column = rank_y * columns + lane_index(rows, columns) - anchor[1]
    covered = (
        (row >= 0) & (row < size_x * span) & (column >= 0) & (column < size_y * (columns // 3))
    )
    first = anchor[0] - (rows - span) * rank_x
    row_shift = lax.rem(first + size_x * rows, rows)
    slab_row = row_index(span, columns)

    def body(ch, carry):
        tiles = []
        for tile in range(3):
            value = None
            for d, slab in zip(shifts, slabs):
                if d % 3 != tile:
                    continue
                other = slab[pl.ds(pl.multiple_of(span * ch, 8), span), :]
                place = first + span * d + slab_row
                inside = (place >= 0) & (place < rows)
                value = other if value is None else jnp.where(inside, other, value)
            tiles.append(value)
        moved = pltpu.roll(jnp.concatenate(tiles, axis=0), row_shift, 0)
        fed_back = pltpu.roll(moved, shift, 1)
        merged[ch] = jnp.where(covered, fed_back, parent_next[ch])
        return carry

    lax.fori_loop(0, channels, body, 0)


def spread_matrix(columns):
    span = columns // 3
    matrix = np.zeros((2 * LANES, columns + LANES), np.float32)

    def source(m):
        return LANES if m < 0 else (LANES + 1 if m >= span else m)

    for c in range(-2, columns + 2):
        m, j = divmod(c, 3)
        at = c % (columns + LANES)
        if j == 0:
            matrix[source(m - 1), at] += 1.0
            matrix[source(m), at] += 2.0
        elif j == 1:
            matrix[source(m), at] += 3.0
        else:
            matrix[source(m), at] += 2.0
            matrix[source(m + 1), at] += 1.0
    return jnp.asarray(matrix, jnp.bfloat16)


def gather_matrix(columns):
    matrix = np.zeros((columns, columns // 3), np.float32)
    matrix[np.arange(columns), np.arange(columns) // 3] = 1.0
    return jnp.asarray(matrix, jnp.bfloat16)


def row_routes(size, rows):
    span = rows // 3
    routes = {}
    for start in range(size * (rows - span) - 2):
        for nest in range(size):
            for at in (start + span * nest, start + span * nest + span + 1):
                routes.setdefault(nest - at // rows, set()).add((at // rows, nest))
    return {d: sorted(pairs) for d, pairs in sorted(routes.items())}


def column_routes(size):
    routes = {}
    for k in (0, 1, -1, 2, -2):
        pairs = [(size // 2 + p, 3 * p + k) for p in range(size - size // 2)]
        routes[k] = [(s, n) for s, n in pairs if 0 <= n < size]
    return routes


def per_device(
    parent_fields,
    parent_velocity,
    parent_mixing,
    nest_fields,
    nest_velocity,
    nest_mixing,
    nest_anchor,
):
    fields, levels, rows, columns = parent_fields.shape
    channels = fields * levels
    span = rows // 3
    gx, gy = lax.axis_size("gx"), lax.axis_size("gy")
    pf = parent_fields.reshape(channels, rows, columns)
    nf = nest_fields.reshape(channels, rows, columns)
    pv = parent_velocity.reshape(2 * levels, rows, columns)
    nv = nest_velocity.reshape(2 * levels, rows, columns)
    pm, nm = parent_mixing, nest_mixing

    halo_rows = 4 * channels + 6 * levels
    rows_next, rows_prev, cols_next, cols_prev = call(
        pack_kernel,
        [(halo_rows, columns)] * 2 + [(rows, LANES)] * 2,
        [pf, nf, nv, nm],
    )
    top, bottom = halo_exchange("gx", rows_next, rows_prev)
    left, right = halo_exchange("gy", cols_next, cols_prev)

    routes = row_routes(gx, rows)
    shifts = tuple(routes)
    slab_shape = ((span + 2) * channels, columns)
    parent_next, *slabs = call(
        parent_kernel,
        [(channels, rows, columns)] + [slab_shape] * 3,
        [nest_anchor, pf, pv, pm, top, bottom, left, right],
        smem=1,
    )
    slabs = [
        slabs[0] if d == 0 else lax.ppermute(slabs[d % 3], "gx", routes[d]) for d in shifts
    ]
    nest_cols_next, nest_cols_prev = call(
        nest_columns_kernel,
        [(rows + 8, LANES)] * 2,
        [nf, nv, nm, top, bottom],
        scratch=[pltpu.VMEM((rows + 8, LANES), F32)],
    )
    nest_left, nest_right = halo_exchange("gy", nest_cols_next, nest_cols_prev)
    message_rows = -(-(span + 2) * (channels + 1) // 8) * 8
    message_rows = -(-message_rows // 16) * 16
    messages = call(
        functools.partial(row_select_kernel, shifts, rows),
        [(message_rows, LANES)] * 3,
        [nest_anchor, *slabs],
        smem=1,
    )
    columns_of = column_routes(gy)
    ks = tuple(columns_of)
    received = [lax.ppermute(messages[k % 3], "gy", columns_of[k]) for k in ks]
    height, width = rows + 8, columns + LANES
    nest_result, coarse = call(
        functools.partial(nest_kernel, ks),
        [(channels, rows, columns), (span * channels, columns // 3)],
        [
            nest_anchor,
            spread_matrix(columns),
            gather_matrix(columns),
            nf,
            nv,
            nm,
            top,
            bottom,
            nest_left,
            nest_right,
            *received,
        ],
        smem=1,
        scratch=[
            pltpu.VMEM((message_rows, 2 * LANES), F32),
            pltpu.VMEM((message_rows, width), F32),
            pltpu.VMEM((width // LANES, height, LANES), F32),
            pltpu.VMEM((height, width), F32),
            pltpu.VMEM((5, height, width), F32),
            pltpu.VMEM((height, width), F32),
            pltpu.VMEM((span * channels, columns), F32),
            pltpu.VMEM((columns // LANES, rows, LANES), F32),
        ],
    )
    returned = [lax.ppermute(coarse, "gy", [(n, s) for s, n in columns_of[k]]) for k in ks]
    placed = call(
        functools.partial(column_select_kernel, ks, columns),
        [(span * channels, columns)],
        [nest_anchor, *returned],
        smem=1,
    )[0]
    fed_back = [
        placed if d == 0 else lax.ppermute(placed, "gx", [(n, s) for s, n in routes[d]])
        for d in shifts
    ]
    merged = call(
        functools.partial(merge_kernel, shifts),
        [(channels, rows, columns)],
        [nest_anchor, parent_next, *fed_back],
        smem=1,
    )[0]
    shape = parent_fields.shape
    return merged.reshape(shape), nest_result.reshape(shape)


def solution(mesh):
    placed = (
        P(None, None, "gx", "gy"),
        P(None, None, "gx", "gy"),
        P(None, "gx", "gy"),
        P(None, None, "gx", "gy"),
        P(None, None, "gx", "gy"),
        P(None, "gx", "gy"),
        P(),
    )
    return jax.shard_map(
        per_device,
        mesh=mesh,
        in_specs=placed,
        out_specs=(P(None, None, "gx", "gy"), P(None, None, "gx", "gy")),
        check_vma=False,
    )
```

time: 558 us -> 138 us (0.25)
  the two profiles are of different devices: /device:TPU:1 before, /device:TPU:23 now
where the time goes in v1:
time: 138 us; the launch traced here: 137 us
  starting transfers between devices  48.7 us (35%)
  waiting for transfers between devices  45.6 us (33%)
  Pallas kernels  37.1 us (27%)
  local copies, waits for them, and re-layouts  4.56 us (3%)
    pallas_call x7, Pallas kernels, call(): pl.pallas_call(body, out_shape=[jax.ShapeDtypeStruct(shape, F32) for shap...  37.1 us
    ppermute x4, waiting for transfers between devices, per_device(): lax.ppermute(placed, 'gx', [(n, s) for s, n in routes[d]])  17.6 us
    ppermute x4, starting transfers between devices, per_device(): lax.ppermute(slabs[d % 3], 'gx', routes[d])  11 us
    ppermute x5, waiting for transfers between devices, per_device(): lax.ppermute(coarse, 'gy', [(n, s) for s, n in columns_of[k]])  10.5 us
    ppermute x3, starting transfers between devices, halo_exchange(): lax.ppermute(to_previous, axis, [(i + 1, i) for i in range(ends)])  8.38 us
    ppermute x5, starting transfers between devices, per_device(): received = [lax.ppermute(messages[k % 3], 'gy', columns_of[k]) for k in ks]  8.05 us
    ppermute x5, waiting for transfers between devices, per_device(): received = [lax.ppermute(messages[k % 3], 'gy', columns_of[k]) for k in ks]  7.57 us
    ppermute x5, starting transfers between devices, per_device(): lax.ppermute(coarse, 'gy', [(n, s) for s, n in columns_of[k]])  7.35 us
  transfers between devices with their start and end apart: 24, of which 9 were waited for; matrix products, arithmetic and copies ran while one was open for 0% of the time, Pallas kernels for 4%

profile of v1, /device:TPU:23, one launch (start us, length us, event | category | flops | bytes accessed | tf_op | source)
XLA Modules:
  0.0 136.9 jit_solution(9336853722489199303)
XLA Ops:
  0.6 3.0 %shard_map.104 = (f32[104,384]{1,0:T(8,128)}, f32[104,384]{1,0:T(8,128)}, f32[48,128]{1,0:T(8,128)}, f32[48,128]{1,0:T(8,128)}) custom-call(f32[20,48,384]{2,1,0:T(8,128)} %bitcast.9, f32[20,48,384]{2,1,0:T(8,128)} %bitcast.6, f32[8,48,384]{2,1,0:T(8,128)} %bitcast.11, f32[4,48,384]{2,1,0:T(8,128)} %nm.5), custom_call_target="tpu_custom_call" | custom-call | tf_op jit(solution)/shard_map/pallas_call | solution.py:23
  5.0 3.2 %collective-permute-start.1 = (f32[104,384]{1,0:T(8,128)}, f32[104,384]{1,0:T(8,128)S(1)}, u32[]{:S(2)}, u32[]{:S(2)}) collective-permute-start(f32[104,384]{1,0:T(8,128)} %get-tuple-element.18), channel_id=1, source_target_pairs={{8,0},{16,8},{24,16},{9,1},{17,9},{25,17},{10,2},{18,10},{26,18},{... | collective-permute-start | bytes 479240 | tf_op jit(solution)/shard_map/ppermute | solution.py:44
  8.2 3.1 %collective-permute-start.2 = (f32[48,128]{1,0:T(8,128)}, f32[48,128]{1,0:T(8,128)S(1)}, u32[]{:S(2)}, u32[]{:S(2)}) collective-permute-start(f32[48,128]{1,0:T(8,128)} %get-tuple-element.19), channel_id=1, source_target_pairs={{0,1},{1,2},{2,3},{3,4},{4,5},{5,6},{6,7},{8,9},{9,10},{10,11},{11... | collective-permute-start | bytes 73736 | tf_op jit(solution)/shard_map/ppermute | solution.py:43
  11.3 2.1 %collective-permute-start.3 = (f32[48,128]{1,0:T(8,128)}, f32[48,128]{1,0:T(8,128)S(1)}, u32[]{:S(2)}, u32[]{:S(2)}) collective-permute-start(f32[48,128]{1,0:T(8,128)} %get-tuple-element.20), channel_id=1, source_target_pairs={{1,0},{2,1},{3,2},{4,3},{5,4},{6,5},{7,6},{9,8},{10,9},{11,10},{12... | collective-permute-start | bytes 73736 | tf_op jit(solution)/shard_map/ppermute | solution.py:44
  13.5 3.5 %collective-permute-done.3.right = f32[48,128]{1,0:T(8,128)S(1)} collective-permute-done((f32[48,128]{1,0:T(8,128)}, f32[48,128]{1,0:T(8,128)S(1)}, u32[]{:S(2)}, u32[]{:S(2)}) %collective-permute-start.3) | collective-permute-done | bytes 24608 | tf_op jit(solution)/shard_map/ppermute | solution.py:44
  17.8 8.0 %shard_map.105 = (f32[20,48,384]{2,1,0:T(8,128)}, f32[360,384]{1,0:T(8,128)}, f32[360,384]{1,0:T(8,128)}, f32[360,384]{1,0:T(8,128)}) custom-call(s32[2]{0:T(128)} %anchor.9, f32[20,48,384]{2,1,0:T(8,128)} %bitcast.10, f32[8,48,384]{2,1,0:T(8,128)} %bitcast.15, f32[4,48,384]{2,1,0:T(8,128)} %pm.1, f32[104,384]{1,0:T(8,128)} %copy-done, ...), custom_call_target="tpu_custom_call" | custom-call | tf_op jit(solution)/shard_map/pallas_call | solution.py:23
  27.1 7.1 %collective-permute-start.6 = (f32[360,384]{1,0:T(8,128)}, f32[360,384]{1,0:T(8,128)S(1)}, u32[]{:S(2)}, u32[]{:S(2)}) collective-permute-start(f32[360,384]{1,0:T(8,128)} %get-tuple-element.24), channel_id=1, source_target_pairs={{16,0},{24,8},{17,1},{25,9},{18,2},{26,10},{19,3},{27,11},{20,4},{... | collective-permute-start | bytes 1658888 | tf_op jit(solution)/shard_map/ppermute | solution.py:534
  36.8 2.9 %shard_map.106 = (f32[56,128]{1,0:T(8,128)}, f32[56,128]{1,0:T(8,128)}) custom-call(f32[20,48,384]{2,1,0:T(8,128)} %bitcast.7, f32[8,48,384]{2,1,0:T(8,128)} %bitcast.12, f32[4,48,384]{2,1,0:T(8,128)} %nm.5, f32[104,384]{1,0:T(8,128)} %copy-done, f32[104,384]{1,0:T(8,128)} %copy-done.1), custom_call_target="tpu_custom_call" | custom-call | tf_op jit(solution)/shard_map/pallas_call | solution.py:23
  39.7 2.2 %collective-permute-start.4 = (f32[56,128]{1,0:T(8,128)}, f32[56,128]{1,0:T(8,128)S(1)}, u32[]{:S(2)}, u32[]{:S(2)}) collective-permute-start(f32[56,128]{1,0:T(8,128)} %get-tuple-element.22), channel_id=1, source_target_pairs={{0,1},{1,2},{2,3},{3,4},{4,5},{5,6},{6,7},{8,9},{9,10},{10,11},{11... | collective-permute-start | bytes 86024 | tf_op jit(solution)/shard_map/ppermute | solution.py:43
  42.0 3.0 %collective-permute-start.5 = (f32[56,128]{1,0:T(8,128)}, f32[56,128]{1,0:T(8,128)S(1)}, u32[]{:S(2)}, u32[]{:S(2)}) collective-permute-start(f32[56,128]{1,0:T(8,128)} %get-tuple-element.23), channel_id=1, source_target_pairs={{1,0},{2,1},{3,2},{4,3},{5,4},{6,5},{7,6},{9,8},{10,9},{11,10},{12... | collective-permute-start | bytes 86024 | tf_op jit(solution)/shard_map/ppermute | solution.py:44
  46.8 4.6 %collective-permute-done.9.refs_4_ = f32[360,384]{1,0:T(8,128)S(1)} collective-permute-done((f32[360,384]{1,0:T(8,128)}, f32[360,384]{1,0:T(8,128)S(1)}, u32[]{:S(2)}, u32[]{:S(2)}) %collective-permute-start.9) | collective-permute-done | bytes 552992 | tf_op jit(solution)/shard_map/ppermute | solution.py:534
  52.4 2.9 %shard_map.107 = (f32[384,128]{1,0:T(8,128)}, f32[384,128]{1,0:T(8,128)}, f32[384,128]{1,0:T(8,128)}) custom-call(s32[2]{0:T(128)} %anchor.9, f32[360,384]{1,0:T(8,128)} %copy-done.3, f32[360,384]{1,0:T(8,128)} %copy-done.5, f32[360,384]{1,0:T(8,128)} %get-tuple-element.26.refs_2_, f32[360,384]{1,0:T(8,128)} %copy-done.2, f32[360,384]{1,0:T(8,128)} %copy-done.4), custom_call_target="tpu_custom_call" | custom-call | tf_op jit(solution)/shard_map/pallas_call | solution.py:23
  55.3 2.0 %collective-permute-start.14 = (f32[384,128]{1,0:T(8,128)}, f32[384,128]{1,0:T(8,128)S(1)}, u32[]{:S(2)}, u32[]{:S(2)}) collective-permute-start(f32[384,128]{1,0:T(8,128)} %get-tuple-element.28), channel_id=1, source_target_pairs={{5,1},{6,4},{7,7},{13,9},{14,12},{15,15},{21,17},{22,20},{23,23},{... | collective-permute-start | bytes 589832 | tf_op jit(solution)/shard_map/ppermute | solution.py:553
  61.5 1.9 %collective-permute-start.12 = (f32[384,128]{1,0:T(8,128)}, f32[384,128]{1,0:T(8,128)S(1)}, u32[]{:S(2)}, u32[]{:S(2)}) collective-permute-start(f32[384,128]{1,0:T(8,128)} %get-tuple-element.29), channel_id=1, source_target_pairs={{5,2},{6,5},{13,10},{14,13},{21,18},{22,21},{29,26},{30,29}} | collective-permute-start | bytes 589832 | tf_op jit(solution)/shard_map/ppermute | solution.py:553
  63.5 2.9 %collective-permute-done.10.refs_0_ = f32[384,128]{1,0:T(8,128)S(1)} collective-permute-done((f32[384,128]{1,0:T(8,128)}, f32[384,128]{1,0:T(8,128)S(1)}, u32[]{:S(2)}, u32[]{:S(2)}) %collective-permute-start.10) | collective-permute-done | bytes 196640 | tf_op jit(solution)/shard_map/ppermute | solution.py:553
  66.4 4.7 %collective-permute-done.12.refs_2_ = f32[384,128]{1,0:T(8,128)S(1)} collective-permute-done((f32[384,128]{1,0:T(8,128)}, f32[384,128]{1,0:T(8,128)S(1)}, u32[]{:S(2)}, u32[]{:S(2)}) %collective-permute-start.12) | collective-permute-done | bytes 196640 | tf_op jit(solution)/shard_map/ppermute | solution.py:553
  71.8 12.7 %shard_map.108 = (f32[20,48,384]{2,1,0:T(8,128)}, f32[320,128]{1,0:T(8,128)}) custom-call(s32[2]{0:T(128)} %anchor.9, bf16[256,512]{1,0:T(8,128)(2,1)} %constant.4.clone.spread, bf16[384,128]{1,0:T(8,128)(2,1)} %constant.5.clone.gather, f32[20,48,384]{2,1,0:T(8,128)} %bitcast.8, f32[8,48,384]{2,1,0:T(8,128)} %bitcast.13, f32[4,48,384]{2,1,0:T(8,128)} %nm.5, ...), custom_call_target="tpu_custom_call" | custom-call | tf_op jit(solution)/shard_map/pallas_call | solution.py:23
  87.3 1.9 %collective-permute-start.17 = (f32[320,128]{1,0:T(8,128)}, f32[320,128]{1,0:T(8,128)S(1)}, u32[]{:S(2)}, u32[]{:S(2)}) collective-permute-start(f32[320,128]{1,0:T(8,128)} %get-tuple-element.30), channel_id=1, source_target_pairs={{2,5},{5,6},{10,13},{13,14},{18,21},{21,22},{26,29},{29,30}} | collective-permute-start | bytes 491528 | tf_op jit(solution)/shard_map/ppermute | solution.py:583
  92.4 10.0 %collective-permute-done.17.refs_2_ = f32[320,128]{1,0:T(8,128)S(1)} collective-permute-done((f32[320,128]{1,0:T(8,128)}, f32[320,128]{1,0:T(8,128)S(1)}, u32[]{:S(2)}, u32[]{:S(2)}) %collective-permute-start.17) | collective-permute-done | bytes 163872 | tf_op jit(solution)/shard_map/ppermute | solution.py:583
  103.8 2.1 %shard_map.109.refs_2_ = f32[320,384]{1,0:T(8,128)} custom-call(s32[2]{0:T(128)} %anchor.9, f32[320,128]{1,0:T(8,128)} %copy-done.19, f32[320,128]{1,0:T(8,128)} %copy-done.18, f32[320,128]{1,0:T(8,128)} %copy-done.17, f32[320,128]{1,0:T(8,128)} %copy-done.16, f32[320,128]{1,0:T(8,128)} %copy-done.15), custom_call_target="tpu_custom_call" | custom-call | tf_op jit(solution)/shard_map/pallas_call | solution.py:23
  107.2 3.4 %collective-permute-start.22 = (f32[320,384]{1,0:T(8,128)}, f32[320,384]{1,0:T(8,128)S(1)}, u32[]{:S(2)}, u32[]{:S(2)}) collective-permute-start(f32[320,384]{1,0:T(8,128)} %shard_map.109.refs_2_), channel_id=1, source_target_pairs={{8,0},{16,8},{24,16},{9,1},{17,9},{25,17},{10,2},{18,10},{26,18},{... | collective-permute-start | bytes 1474568 | tf_op jit(solution)/shard_map/ppermute | solution.py:591
  113.2 3.6 %collective-permute-done.23.refs_4_ = f32[320,384]{1,0:T(8,128)S(1)} collective-permute-done((f32[320,384]{1,0:T(8,128)}, f32[320,384]{1,0:T(8,128)S(1)}, u32[]{:S(2)}, u32[]{:S(2)}) %collective-permute-start.23) | collective-permute-done | bytes 491552 | tf_op jit(solution)/shard_map/ppermute | solution.py:591
  116.8 13.9 %collective-permute-done.20.refs_0_ = f32[320,384]{1,0:T(8,128)S(1)} collective-permute-done((f32[320,384]{1,0:T(8,128)}, f32[320,384]{1,0:T(8,128)S(1)}, u32[]{:S(2)}, u32[]{:S(2)}) %collective-permute-start.20) | collective-permute-done | bytes 491552 | tf_op jit(solution)/shard_map/ppermute | solution.py:591
  131.6 5.4 %shard_map.110 = f32[20,48,384]{2,1,0:T(8,128)} custom-call(s32[2]{0:T(128)} %anchor.9, f32[20,48,384]{2,1,0:T(8,128)} %get-tuple-element.21.parent_next, f32[320,384]{1,0:T(8,128)} %copy-done.9, f32[320,384]{1,0:T(8,128)} %copy-done.8, f32[320,384]{1,0:T(8,128)} %shard_map.109.refs_2_, f32[320,384]{1,0:T(8,128)} %copy-done.7, f32[320,384]{1,0:T(8,128)} %copy-done.6), custom_call_target="tpu_custom_call" | custom-call | tf_op jit(solution)/shard_map/pallas_call | solution.py:23
  (79 shorter events, 25.7 us)
Async XLA Ops:
  3.7 13.4 %collective-permute-start = (f32[104,384]{1,0:T(8,128)}, f32[104,384]{1,0:T(8,128)S(1)}, u32[]{:S(2)}, u32[]{:S(2)}) collective-permute-start(f32[104,384]{1,0:T(8,128)} %get-tuple-element.17), channel_id=1, source_target_pairs={{0,8},{8,16},{16,24},{1,9},{9,17},{17,25},{2,10},{10,18},{18,26},{... | collective-permute-start | bytes 479240 | tf_op jit(solution)/shard_map/ppermute | solution.py:43
  5.0 12.1 %collective-permute-start.1 = (f32[104,384]{1,0:T(8,128)}, f32[104,384]{1,0:T(8,128)S(1)}, u32[]{:S(2)}, u32[]{:S(2)}) collective-permute-start(f32[104,384]{1,0:T(8,128)} %get-tuple-element.18), channel_id=1, source_target_pairs={{8,0},{16,8},{24,16},{9,1},{17,9},{25,17},{10,2},{18,10},{26,18},{... | collective-permute-start | bytes 479240 | tf_op jit(solution)/shard_map/ppermute | solution.py:44
  8.2 5.3 %collective-permute-start.2 = (f32[48,128]{1,0:T(8,128)}, f32[48,128]{1,0:T(8,128)S(1)}, u32[]{:S(2)}, u32[]{:S(2)}) collective-permute-start(f32[48,128]{1,0:T(8,128)} %get-tuple-element.19), channel_id=1, source_target_pairs={{0,1},{1,2},{2,3},{3,4},{4,5},{5,6},{6,7},{8,9},{9,10},{10,11},{11... | collective-permute-start | bytes 73736 | tf_op jit(solution)/shard_map/ppermute | solution.py:43
  11.3 5.7 %collective-permute-start.3 = (f32[48,128]{1,0:T(8,128)}, f32[48,128]{1,0:T(8,128)S(1)}, u32[]{:S(2)}, u32[]{:S(2)}) collective-permute-start(f32[48,128]{1,0:T(8,128)} %get-tuple-element.20), channel_id=1, source_target_pairs={{1,0},{2,1},{3,2},{4,3},{5,4},{6,5},{7,6},{9,8},{10,9},{11,10},{12... | collective-permute-start | bytes 73736 | tf_op jit(solution)/shard_map/ppermute | solution.py:44
  25.8 16.2 %collective-permute-start.8 = (f32[360,384]{1,0:T(8,128)}, f32[360,384]{1,0:T(8,128)S(1)}, u32[]{:S(2)}, u32[]{:S(2)}) collective-permute-start(f32[360,384]{1,0:T(8,128)} %get-tuple-element.24), channel_id=1, source_target_pairs={{0,8},{8,16},{16,24},{1,9},{9,17},{17,25},{2,10},{10,18},{18,26},{... | collective-permute-start | bytes 1658888 | tf_op jit(solution)/shard_map/ppermute | solution.py:534
  27.1 19.8 %collective-permute-start.6 = (f32[360,384]{1,0:T(8,128)}, f32[360,384]{1,0:T(8,128)S(1)}, u32[]{:S(2)}, u32[]{:S(2)}) collective-permute-start(f32[360,384]{1,0:T(8,128)} %get-tuple-element.24), channel_id=1, source_target_pairs={{16,0},{24,8},{17,1},{25,9},{18,2},{26,10},{19,3},{27,11},{20,4},{... | collective-permute-start | bytes 1658888 | tf_op jit(solution)/shard_map/ppermute | solution.py:534
  34.1 17.3 %collective-permute-start.9 = (f32[360,384]{1,0:T(8,128)}, f32[360,384]{1,0:T(8,128)S(1)}, u32[]{:S(2)}, u32[]{:S(2)}) collective-permute-start(f32[360,384]{1,0:T(8,128)} %get-tuple-element.25), channel_id=1, source_target_pairs={{0,16},{8,24},{1,17},{9,25},{2,18},{10,26},{3,19},{11,27},{4,20},{... | collective-permute-start | bytes 1658888 | tf_op jit(solution)/shard_map/ppermute | solution.py:534
  35.4 16.0 %collective-permute-start.7 = (f32[360,384]{1,0:T(8,128)}, f32[360,384]{1,0:T(8,128)S(1)}, u32[]{:S(2)}, u32[]{:S(2)}) collective-permute-start(f32[360,384]{1,0:T(8,128)} %get-tuple-element.25), channel_id=1, source_target_pairs={{8,0},{16,8},{24,16},{9,1},{17,9},{25,17},{10,2},{18,10},{26,18},{... | collective-permute-start | bytes 1658888 | tf_op jit(solution)/shard_map/ppermute | solution.py:534
  39.7 20.2 %collective-permute-start.4 = (f32[56,128]{1,0:T(8,128)}, f32[56,128]{1,0:T(8,128)S(1)}, u32[]{:S(2)}, u32[]{:S(2)}) collective-permute-start(f32[56,128]{1,0:T(8,128)} %get-tuple-element.22), channel_id=1, source_target_pairs={{0,1},{1,2},{2,3},{3,4},{4,5},{5,6},{6,7},{8,9},{9,10},{10,11},{11... | collective-permute-start | bytes 86024 | tf_op jit(solution)/shard_map/ppermute | solution.py:43
  42.0 19.6 %collective-permute-start.5 = (f32[56,128]{1,0:T(8,128)}, f32[56,128]{1,0:T(8,128)S(1)}, u32[]{:S(2)}, u32[]{:S(2)}) collective-permute-start(f32[56,128]{1,0:T(8,128)} %get-tuple-element.23), channel_id=1, source_target_pairs={{1,0},{2,1},{3,2},{4,3},{5,4},{6,5},{7,6},{9,8},{10,9},{11,10},{12... | collective-permute-start | bytes 86024 | tf_op jit(solution)/shard_map/ppermute | solution.py:44
  55.3 11.0 %collective-permute-start.14 = (f32[384,128]{1,0:T(8,128)}, f32[384,128]{1,0:T(8,128)S(1)}, u32[]{:S(2)}, u32[]{:S(2)}) collective-permute-start(f32[384,128]{1,0:T(8,128)} %get-tuple-element.28), channel_id=1, source_target_pairs={{5,1},{6,4},{7,7},{13,9},{14,12},{15,15},{21,17},{22,20},{23,23},{... | collective-permute-start | bytes 589832 | tf_op jit(solution)/shard_map/ppermute | solution.py:553
  57.3 9.0 %collective-permute-start.11 = (f32[384,128]{1,0:T(8,128)}, f32[384,128]{1,0:T(8,128)S(1)}, u32[]{:S(2)}, u32[]{:S(2)}) collective-permute-start(f32[384,128]{1,0:T(8,128)} %get-tuple-element.28), channel_id=1, source_target_pairs={{4,1},{5,4},{6,7},{12,9},{13,12},{14,15},{20,17},{21,20},{22,23},{... | collective-permute-start | bytes 589832 | tf_op jit(solution)/shard_map/ppermute | solution.py:553
  58.6 7.7 %collective-permute-start.10 = (f32[384,128]{1,0:T(8,128)}, f32[384,128]{1,0:T(8,128)S(1)}, u32[]{:S(2)}, u32[]{:S(2)}) collective-permute-start(f32[384,128]{1,0:T(8,128)} %get-tuple-element.27), channel_id=1, source_target_pairs={{4,0},{5,3},{6,6},{12,8},{13,11},{14,14},{20,16},{21,19},{22,22},{... | collective-permute-start | bytes 589832 | tf_op jit(solution)/shard_map/ppermute | solution.py:553
  60.0 6.4 %collective-permute-start.13 = (f32[384,128]{1,0:T(8,128)}, f32[384,128]{1,0:T(8,128)S(1)}, u32[]{:S(2)}, u32[]{:S(2)}) collective-permute-start(f32[384,128]{1,0:T(8,128)} %get-tuple-element.29), channel_id=1, source_target_pairs={{4,2},{5,5},{12,10},{13,13},{20,18},{21,21},{28,26},{29,29}} | collective-permute-start | bytes 589832 | tf_op jit(solution)/shard_map/ppermute | solution.py:553
  61.5 9.5 %collective-permute-start.12 = (f32[384,128]{1,0:T(8,128)}, f32[384,128]{1,0:T(8,128)S(1)}, u32[]{:S(2)}, u32[]{:S(2)}) collective-permute-start(f32[384,128]{1,0:T(8,128)} %get-tuple-element.29), channel_id=1, source_target_pairs={{5,2},{6,5},{13,10},{14,13},{21,18},{22,21},{29,26},{30,29}} | collective-permute-start | bytes 589832 | tf_op jit(solution)/shard_map/ppermute | solution.py:553
  84.5 7.9 %collective-permute-start.19 = (f32[320,128]{1,0:T(8,128)}, f32[320,128]{1,0:T(8,128)S(1)}, u32[]{:S(2)}, u32[]{:S(2)}) collective-permute-start(f32[320,128]{1,0:T(8,128)} %get-tuple-element.30), channel_id=1, source_target_pairs={{1,5},{4,6},{7,7},{9,13},{12,14},{15,15},{17,21},{20,22},{23,23},{... | collective-permute-start | bytes 491528 | tf_op jit(solution)/shard_map/ppermute | solution.py:583
  85.8 6.6 %collective-permute-start.18 = (f32[320,128]{1,0:T(8,128)}, f32[320,128]{1,0:T(8,128)S(1)}, u32[]{:S(2)}, u32[]{:S(2)}) collective-permute-start(f32[320,128]{1,0:T(8,128)} %get-tuple-element.30), channel_id=1, source_target_pairs={{2,4},{5,5},{10,12},{13,13},{18,20},{21,21},{26,28},{29,29}} | collective-permute-start | bytes 491528 | tf_op jit(solution)/shard_map/ppermute | solution.py:583
  87.3 15.1 %collective-permute-start.17 = (f32[320,128]{1,0:T(8,128)}, f32[320,128]{1,0:T(8,128)S(1)}, u32[]{:S(2)}, u32[]{:S(2)}) collective-permute-start(f32[320,128]{1,0:T(8,128)} %get-tuple-element.30), channel_id=1, source_target_pairs={{2,5},{5,6},{10,13},{13,14},{18,21},{21,22},{26,29},{29,30}} | collective-permute-start | bytes 491528 | tf_op jit(solution)/shard_map/ppermute | solution.py:583
  89.3 13.1 %collective-permute-start.16 = (f32[320,128]{1,0:T(8,128)}, f32[320,128]{1,0:T(8,128)S(1)}, u32[]{:S(2)}, u32[]{:S(2)}) collective-permute-start(f32[320,128]{1,0:T(8,128)} %get-tuple-element.30), channel_id=1, source_target_pairs={{1,4},{4,5},{7,6},{9,12},{12,13},{15,14},{17,20},{20,21},{23,22},{... | collective-permute-start | bytes 491528 | tf_op jit(solution)/shard_map/ppermute | solution.py:583
  90.6 11.9 %collective-permute-start.15 = (f32[320,128]{1,0:T(8,128)}, f32[320,128]{1,0:T(8,128)S(1)}, u32[]{:S(2)}, u32[]{:S(2)}) collective-permute-start(f32[320,128]{1,0:T(8,128)} %get-tuple-element.30), channel_id=1, source_target_pairs={{0,4},{3,5},{6,6},{8,12},{11,13},{14,14},{16,20},{19,21},{22,22},{... | collective-permute-start | bytes 491528 | tf_op jit(solution)/shard_map/ppermute | solution.py:583
  105.9 10.9 %collective-permute-start.23 = (f32[320,384]{1,0:T(8,128)}, f32[320,384]{1,0:T(8,128)S(1)}, u32[]{:S(2)}, u32[]{:S(2)}) collective-permute-start(f32[320,384]{1,0:T(8,128)} %shard_map.109.refs_2_), channel_id=1, source_target_pairs={{16,0},{24,8},{17,1},{25,9},{18,2},{26,10},{19,3},{27,11},{20,4},{... | collective-permute-start | bytes 1474568 | tf_op jit(solution)/shard_map/ppermute | solution.py:591
  107.2 9.6 %collective-permute-start.22 = (f32[320,384]{1,0:T(8,128)}, f32[320,384]{1,0:T(8,128)S(1)}, u32[]{:S(2)}, u32[]{:S(2)}) collective-permute-start(f32[320,384]{1,0:T(8,128)} %shard_map.109.refs_2_), channel_id=1, source_target_pairs={{8,0},{16,8},{24,16},{9,1},{17,9},{25,17},{10,2},{18,10},{26,18},{... | collective-permute-start | bytes 1474568 | tf_op jit(solution)/shard_map/ppermute | solution.py:591
  110.6 6.2 %collective-permute-start.21 = (f32[320,384]{1,0:T(8,128)}, f32[320,384]{1,0:T(8,128)S(1)}, u32[]{:S(2)}, u32[]{:S(2)}) collective-permute-start(f32[320,384]{1,0:T(8,128)} %shard_map.109.refs_2_), channel_id=1, source_target_pairs={{0,8},{8,16},{16,24},{1,9},{9,17},{17,25},{2,10},{10,18},{18,26},{... | collective-permute-start | bytes 1474568 | tf_op jit(solution)/shard_map/ppermute | solution.py:591
  111.9 18.9 %collective-permute-start.20 = (f32[320,384]{1,0:T(8,128)}, f32[320,384]{1,0:T(8,128)S(1)}, u32[]{:S(2)}, u32[]{:S(2)}) collective-permute-start(f32[320,384]{1,0:T(8,128)} %shard_map.109.refs_2_), channel_id=1, source_target_pairs={{0,16},{8,24},{1,17},{9,25},{2,18},{10,26},{3,19},{11,27},{4,20},{... | collective-permute-start | bytes 1474568 | tf_op jit(solution)/shard_map/ppermute | solution.py:591
  (24 other events, 126.4 us)

commit v2 on v0

v2 whole, which is shorter than its diff:
```python
import functools

import jax
import jax.numpy as jnp
import numpy as np
from jax import lax
from jax.experimental import pallas as pl
from jax.experimental.pallas import tpu as pltpu
from jax.sharding import PartitionSpec as P

SUBSTEPS = 3
F32 = jnp.float32
LANES = 128
VMEM_LIMIT = 56 * 1024 * 1024
nudge_floor = 0.1
relax_width = 4.0


def whole(array):
    return pl.BlockSpec(array.shape, lambda level: (0,) * array.ndim)


def block(shape, at):
    return pl.BlockSpec(shape, lambda level: at)


def by_level(shape, dim):
    sizes = tuple(1 if i == dim else n for i, n in enumerate(shape))
    return pl.BlockSpec(sizes, lambda level: tuple(level if i == dim else 0 for i in range(len(shape))))


def call(body, grid, ins, outs, scratch=(), cost=None):
    return pl.pallas_call(
        body,
        grid=(grid,),
        out_shape=[jax.ShapeDtypeStruct(shape, F32) for shape, _ in outs],
        in_specs=[spec for _, spec in ins],
        out_specs=[spec for _, spec in outs],
        scratch_shapes=[pltpu.VMEM(shape, F32) for shape in scratch],
        cost_estimate=cost,
        compiler_params=pltpu.CompilerParams(vmem_limit_bytes=VMEM_LIMIT),
    )(*[array for array, _ in ins])


def lane_index(rows, lanes=LANES):
    return lax.broadcasted_iota(jnp.int32, (rows, lanes), 1)


def row_index(rows, lanes=LANES):
    return lax.broadcasted_iota(jnp.int32, (rows, lanes), 0)


def among(value, numbers):
    found = False
    for number in numbers:
        found = found | (value == number)
    return found


def halo_exchange(axis, to_next, to_previous):
    ends = lax.axis_size(axis) - 1
    from_previous = lax.ppermute(to_next, axis, [(i, i + 1) for i in range(ends)])
    from_next = lax.ppermute(to_previous, axis, [(i + 1, i) for i in range(ends)])
    return from_previous, from_next


def pack_kernel(pf_head, pf_tail, pf_first, pf_last, nf_head, nf_tail, nv_head, nv_tail, nm_head, nm_tail, *outs):
    rows_next, rows_prev, cols_next, cols_prev = outs
    channels, rows = pf_first.shape[:2]
    coefs = nv_head.shape[0] + nm_head.shape[0]
    lanes = lane_index(rows)
    last = jnp.zeros((rows, LANES), F32)
    first = jnp.zeros((rows, LANES), F32)
    for ch in range(channels):
        last = jnp.where(lanes == ch, pltpu.roll(pf_last[ch], (ch + 1) % LANES, 1), last)
        first = jnp.where(lanes == ch, pltpu.roll(pf_first[ch], ch, 1), first)
    cols_next[...] = last
    cols_prev[...] = first
    for ch in range(channels):
        for at in range(3):
            here = at * channels + ch
            rows_next[here : here + 1, :] = nf_tail[ch, 5 + at : 6 + at, :]
            rows_prev[here : here + 1, :] = nf_head[ch, at : at + 1, :]
    base = 3 * channels
    for cc in range(coefs):
        wind = cc < nv_head.shape[0]
        tail, head = (nv_tail, nv_head) if wind else (nm_tail, nm_head)
        row = cc if wind else cc - nv_head.shape[0]
        for at in range(2):
            here = base + at * coefs + cc
            rows_next[here : here + 1, :] = tail[row, 6 + at : 7 + at, :]
            rows_prev[here : here + 1, :] = head[row, at : at + 1, :]
    base = base + 2 * coefs
    for ch in range(channels):
        rows_next[base + ch : base + ch + 1, :] = pf_tail[ch, 7:8, :]
        rows_prev[base + ch : base + ch + 1, :] = pf_head[ch, 0:1, :]


def parent_kernel(cuts, anchor, pf, pv, pm, top, bottom, left, right, parent_next, *rest):
    slabs, rims = rest[:-1], rest[-1]
    fields, _, rows, columns = pf.shape
    level, levels = pl.program_id(0), pl.num_programs(0)
    channels = fields * levels
    span = rows // 3
    rank, size_x = lax.axis_index("gx"), lax.axis_size("gx")
    half = lax.axis_size("gy") // 2 * columns
    base = 3 * channels + 2 * 3 * levels
    shift = lax.rem(2 * columns - anchor[1] + half, columns)
    row_shift = lax.rem((rows - span) * rank + size_x * rows - anchor[0], rows)
    row = row_index(rows, columns)
    column = lane_index(rows, columns)
    lanes = lane_index(rows)
    u, v, k = pv[0, 0], pv[1, 0], pm[0]
    a_w = jnp.maximum(u, 0.0) + k
    a_e = k - jnp.minimum(u, 0.0)
    a_s = jnp.maximum(v, 0.0) + k
    a_n = k - jnp.minimum(v, 0.0)
    a_c = 1.0 - (a_w + a_e + a_s + a_n)
    pad = jnp.zeros((rows, columns - LANES), F32)

    @pl.when(level == 0)
    def _():
        rims[...] = jnp.zeros_like(rims)

    packed = [rims[tile] for tile in range(3)]
    for field in range(fields):
        ch = field * levels + level
        q = pf[field, 0]
        west = jnp.where(row == 0, top[pl.ds(base + ch, 1), :], pltpu.roll(q, 1, 0))
        east = jnp.where(
            row == rows - 1, bottom[pl.ds(base + ch, 1), :], pltpu.roll(q, rows - 1, 0)
        )
        at_first = pltpu.roll(left[...], LANES - ch, 1)
        at_last = pltpu.roll(right[...], LANES - 1 - ch, 1)
        south = jnp.where(
            column == 0, jnp.concatenate([at_first, pad], axis=1), pltpu.roll(q, 1, 1)
        )
        north = jnp.where(
            column == columns - 1,
            jnp.concatenate([pad, at_last], axis=1),
            pltpu.roll(q, columns - 1, 1),
        )
        result = a_c * q + a_w * west + a_e * east + a_s * south + a_n * north
        parent_next[field, 0] = result
        moved = pltpu.roll(pltpu.roll(result, shift, 1), row_shift, 0)
        here = level * fields + field
        tiles = [moved[:, LANES * tile : LANES * (tile + 1)] for tile in range(3)]
        for tile in range(3):
            beside = jnp.where(lanes == LANES - 1, tiles[(tile + 2) % 3], tiles[(tile + 1) % 3])
            inside = (lanes == 2 * here) | (lanes == 2 * here + 1)
            packed[tile] = jnp.where(inside, pltpu.roll(beside, 2 * here + 1, 1), packed[tile])
        for kind in range(3):
            first = span * kind
            before, after = (first - 1) % rows, (first + span) % rows
            for cut, (low, high) in enumerate(cuts):
                slab, part = slabs[3 * cut + kind], slice(LANES * low, LANES * high)
                slab[pl.ds(pl.multiple_of(span * here, 8), span), :] = moved[first : first + span, part]
                slab[pl.ds(span * channels + here, 1), :] = moved[before : before + 1, part]
                slab[pl.ds((span + 1) * channels + here, 1), :] = moved[after : after + 1, part]
    for tile in range(3):
        rims[tile] = packed[tile]

    @pl.when(level == levels - 1)
    def _():
        total = (span + 2) * channels
        for kind in range(3):
            first = span * kind
            before, after = (first - 1) % rows, (first + span) % rows
            for cut, (low, high) in enumerate(cuts):
                slab = slabs[3 * cut + kind]
                for tile in range(low, high):
                    part = slice(LANES * (tile - low), LANES * (tile - low + 1))
                    slab[total : total + span, part] = rims[tile, first : first + span]
                    slab[total + span : total + span + 1, part] = rims[tile, before : before + 1]
                    slab[total + span + 1 : total + span + 2, part] = rims[tile, after : after + 1]
                    padding = slab.shape[0] - total - span - 2
                    slab[total + span + 2 :, part] = jnp.zeros((padding, LANES), F32)


def row_select_kernel(entries, rows, channels, anchor, *refs):
    count = len(entries)
    slabs, messages = refs[:count], refs[count:]
    span = rows // 3
    rank = lax.axis_index("gx")
    start = anchor[0] + span * rank
    lowest, highest = lax.div(start, rows), lax.div(start + span - 1, rows)
    above, below = lax.div(start - 1, rows), lax.div(start + span, rows)
    split = jnp.where(highest > lowest, rows * highest - start, span)

    def pick(owner, first, size, part):
        value = slabs[0][first : first + size, part]
        for (d, ranks), slab in zip(entries[1:], slabs[1:]):
            chosen = (rank - owner == d) & among(rank, ranks)
            value = jnp.where(chosen, slab[first : first + size, part], value)
        return value

    for tile, message in enumerate(messages):
        part = slice(LANES * tile, LANES * (tile + 1))
        cells, total = span * channels, (span + 2) * channels
        for first, size in ((0, cells), (total, span)):
            row = row_index(size) & (span - 1)
            low, high = pick(lowest, first, size, part), pick(highest, first, size, part)
            message[first : first + size, :] = jnp.where(row < split, low, high)
        for first, size in ((cells, channels), (total + span, 1)):
            message[first : first + size, :] = pick(above, first, size, part)
            message[first + size : first + 2 * size, :] = pick(below, first + size, size, part)
        message[total + span + 2 :, :] = jnp.zeros((message.shape[0] - total - span - 2, LANES), F32)


def nest_columns_kernel(nf_first, nf_last, nv_first, nv_last, nm_first, nm_last, top, bottom, cols_next, cols_prev):
    channels, rows = nf_first.shape[:2]
    columns = top.shape[1]
    winds = nv_first.shape[0]
    coefs = winds + nm_first.shape[0]
    height = rows + 8
    lanes, lane = lane_index(rows), lane_index(1)

    def packed(out, nf, nv, nm, part, moved):
        main = jnp.zeros((rows, LANES), F32)
        lines = {at: jnp.zeros((1, LANES), F32) for at in range(-3, 3)}

        def add(first, size, tile, halo_rows):
            nonlocal main
            shift = (first + (size if moved else 0)) % LANES
            inside = (lanes >= first) & (lanes < first + size)
            main = jnp.where(inside, pltpu.roll(tile, shift, 1), main)
            inside = (lane >= first) & (lane < first + size)
            for at, value in halo_rows:
                lines[at] = jnp.where(inside, pltpu.roll(value, shift, 1), lines[at])

        def halos(base, step, size, at):
            pairs = []
            for n in range(size):
                here = base + n * step + at
                pairs.append((n, bottom[here : here + 1, part]))
                pairs.append((n - size, top[here : here + 1, part]))
            return pairs

        for ch in range(channels):
            add(3 * ch, 3, nf[ch], halos(0, channels, 3, ch))
        base = 3 * channels
        for cc in range(coefs):
            tile = nv[cc] if cc < winds else nm[cc - winds]
            add(base + 2 * cc, 2, tile, halos(base, coefs, 2, cc))
        out[0:rows, :] = main
        out[rows:height, :] = jnp.zeros((height - rows, LANES), F32)
        for at, line in lines.items():
            target = rows + at if at >= 0 else height + at
            out[target : target + 1, :] = line

    packed(cols_next, nf_last, nv_last, nm_last, slice(columns - LANES, columns), True)
    packed(cols_prev, nf_first, nv_first, nm_first, slice(0, LANES), False)


def three_parts(x):
    high = x.astype(jnp.bfloat16)
    rest = x - high.astype(F32)
    middle = rest.astype(jnp.bfloat16)
    low = (rest - middle.astype(F32)).astype(jnp.bfloat16)
    return high, middle, low


def exact_dot(x, matrix):
    parts = three_parts(x)
    total = jnp.dot(parts[2], matrix, preferred_element_type=F32)
    total = total + jnp.dot(parts[1], matrix, preferred_element_type=F32)
    return total + jnp.dot(parts[0], matrix, preferred_element_type=F32)


def stencil(q, coefs):
    height, width = q.shape
    return (
        coefs[0] * q
        + coefs[1] * pltpu.roll(q, 1, 0)
        + coefs[2] * pltpu.roll(q, height - 1, 0)
        + coefs[3] * pltpu.roll(q, 1, 1)
        + coefs[4] * pltpu.roll(q, width - 1, 1)
    )


def nest_start_kernel(nf, nv, nm, top, bottom, left, right, coefs, moved, weights, state):
    fields, _, rows, columns = nf.shape
    level, levels = pl.program_id(0), pl.num_programs(0)
    channels = fields * levels
    height, width = rows + 8, columns + LANES
    rank_x, rank_y = lax.axis_index("gx"), lax.axis_index("gy")
    row = row_index(height, width)
    column = lane_index(height, width)
    local_row = jnp.where(row < rows + 4, row, row - height)
    local_column = jnp.where(column < columns + LANES // 2, column, column - width)
    global_row = rank_x * rows + local_row
    global_column = rank_y * columns + local_column
    row_distance = jnp.minimum(global_row, lax.axis_size("gx") * rows - 1 - global_row)
    column_distance = jnp.minimum(
        global_column, lax.axis_size("gy") * columns - 1 - global_column
    )
    distance = jnp.minimum(row_distance, column_distance)
    weight = nudge_floor + (1.0 - nudge_floor) * jnp.exp(
        jnp.maximum(distance, 0).astype(F32) / -relax_width
    )
    weight = jnp.where(distance < 0, 0.0, weight)
    keep = 1.0 - weight
    edge_lanes = lane_index(height)

    @pl.when(level == 0)
    def _():
        weights[...] = weight / 9.0
        state[...] = jnp.zeros_like(state)

    def side_tile(first, size):
        after = pltpu.roll(right[...], lax.rem(2 * LANES - first, LANES), 1)
        before = pltpu.roll(left[...], lax.rem(2 * LANES - first - size, LANES), 1)
        inside = jnp.where(edge_lanes < LANES // 2, after, before)
        outside = (edge_lanes >= size) & (edge_lanes < LANES - size)
        return jnp.where(outside, 0.0, inside)

    def fill(slot, value, base, step, at, size, first):
        state[slot, 0:rows, 0:columns] = value
        for n in range(size):
            source = pl.ds(base + n * step + at, 1)
            state[slot, rows + n : rows + n + 1, 0:columns] = bottom[source, :]
            target = height - size + n
            state[slot, target : target + 1, 0:columns] = top[source, :]
        state[slot, :, columns:width] = side_tile(first, size)

    base = 3 * channels
    for slot, value in enumerate((nv[0, 0], nv[1, 0], nm[0])):
        cc = slot * levels + level
        fill(slot + fields, value, base, 3 * levels, cc, 2, base + 2 * cc)
    for field in range(fields):
        ch = field * levels + level
        fill(field, nf[field, 0], 0, channels, ch, 3, 3 * ch)
    u, v, k = (state[slot + fields] for slot in range(3))
    a_w = jnp.maximum(u, 0.0) + k
    a_e = k - jnp.minimum(u, 0.0)
    a_s = jnp.maximum(v, 0.0) + k
    a_n = k - jnp.minimum(v, 0.0)
    a_c = 1.0 - (a_w + a_e + a_s + a_n)
    for slot, value in enumerate((a_c, a_w, a_e, a_s, a_n)):
        coefs[0, slot] = keep * value
    for field in range(fields):
        moved[0, field] = stencil(state[field], [coefs[0, slot] for slot in range(5)])


def nest_kernel(ks, anchor, spread, gather, coefs, moved, weights, *refs):
    count = len(ks)
    received = dict(zip(ks, refs[:count]))
    result, coarse = refs[count : count + 2]
    relay, refined, forcing, state, sums, final = refs[count + 2 :]
    fields, _, rows, columns = result.shape
    level, levels = pl.program_id(0), pl.num_programs(0)
    channels = fields * levels
    span_rows, span_columns = rows // 3, columns // 3
    height, width = rows + 8, columns + LANES
    tiles = width // LANES
    relay_rows = span_rows + 2
    total = relay_rows * channels
    offset = anchor[1] - lax.axis_size("gy") // 2 * columns
    kind = lax.rem(lax.axis_index("gy"), 3)
    edge = columns - offset - span_columns * kind

    @pl.when(level == 0)
    def _():
        lower = jnp.where(kind == 1, received[1][...], received[2][...])
        lower = jnp.where(kind == 0, received[0][...], lower)
        upper = jnp.where(kind == 1, received[-2][...], received[-1][...])
        lanes = lane_index(lower.shape[0])
        relay[:, 0:LANES] = jnp.where(lanes < edge, lower, upper)
        relay[total:, LANES:] = jnp.zeros((relay.shape[0] - total, LANES), F32)
        rim_low, rim_high = lower[total : total + relay_rows], upper[total : total + relay_rows]
        odd = (lane_index(relay_rows) & 1) == 1
        rim = jnp.where(jnp.where(odd, LANES, -1) < edge, rim_low, rim_high)
        for ch in range(channels):
            sides = pltpu.roll(rim, (LANES - 2 * ch) % LANES, 1)
            relay[span_rows * ch : span_rows * (ch + 1), LANES:] = sides[0:span_rows]
            for side in (span_rows, span_rows + 1):
                here = side * channels + ch
                relay[here : here + 1, LANES:] = sides[side : side + 1]
        refined[...] = exact_dot(relay[...], spread[...])

    relay_row = row_index(span_rows, width)
    for field in range(fields):
        ch = level * fields + field
        centre = refined[pl.ds(pl.multiple_of(span_rows * ch, 8), span_rows), :]
        above = refined[pl.ds(span_rows * channels + ch, 1), :]
        below = refined[pl.ds((span_rows + 1) * channels + ch, 1), :]
        before = jnp.where(relay_row == 0, above, pltpu.roll(centre, 1, 0))
        after = jnp.where(
            relay_row == span_rows - 1, below, pltpu.roll(centre, span_rows - 1, 0)
        )
        thirds = (before + 2.0 * centre, 3.0 * centre, 2.0 * centre + after)
        rims = (
            (rows, centre[span_rows - 1 :] + 2.0 * below),
            (rows + 1, 3.0 * below),
            (height - 2, 3.0 * above),
            (height - 1, 2.0 * above + centre[0:1]),
        )
        for tile in range(tiles):
            part = slice(LANES * tile, LANES * (tile + 1))
            for at, value in enumerate(thirds):
                forcing[field, tile, pl.ds(at, span_rows, stride=3), :] = value[:, part]
            forcing[field, tile, rows + 2 : height - 2, :] = jnp.zeros((4, LANES), F32)
            for at, value in rims:
                forcing[field, tile, at : at + 1, :] = value[:, part]
    for field in range(fields):
        for tile in range(tiles):
            part = slice(LANES * tile, LANES * (tile + 1))
            pull = weights[:, part] * forcing[field, tile]
            forcing[field, tile] = pull
            state[field, :, part] = moved[0, field, :, part] + pull
    for _ in range(SUBSTEPS - 1):
        for field in range(fields):
            pull = jnp.concatenate([forcing[field, tile] for tile in range(tiles)], axis=1)
            state[field] = pull + stencil(state[field], [coefs[0, slot] for slot in range(5)])
    for field in range(fields):
        result[field, 0] = state[field, 0:rows, 0:columns]
        for tile in range(tiles - 1):
            part = slice(LANES * tile, LANES * (tile + 1))
            final[field, tile] = state[field, 0:rows, part]
            sums[span_rows * field : span_rows * (field + 1), part] = (
                final[field, tile, pl.ds(0, span_rows, stride=3), :]
                + final[field, tile, pl.ds(1, span_rows, stride=3), :]
                + final[field, tile, pl.ds(2, span_rows, stride=3), :]
            )
    coarse[...] = exact_dot(sums[...], gather[...]) / 9.0


def column_select_kernel(tile, columns, anchor, own, other, placed):
    offset = anchor[1] - lax.axis_size("gy") // 2 * columns
    inside = lane_index(placed.shape[0]) < columns - offset - LANES * tile
    placed[...] = jnp.where(inside, own[...], other[...])


def merge_kernel(entries, anchor, parent_next, *refs):
    merged = refs[-1]
    fields, _, rows, columns = parent_next.shape
    span = rows // 3
    rank_x, rank_y = lax.axis_index("gx"), lax.axis_index("gy")
    size_x, size_y = lax.axis_size("gx"), lax.axis_size("gy")
    offset = anchor[1] - size_y // 2 * columns
    shift = lax.rem(offset + columns, columns)
    row = rank_x * rows + row_index(rows, columns) - anchor[0]
    column = rank_y * columns + lane_index(rows, columns) - anchor[1]
    covered = (
        (row >= 0) & (row < size_x * span) & (column >= 0) & (column < size_y * (columns // 3))
    )
    first = anchor[0] - (rows - span) * rank_x
    row_shift = lax.rem(first + size_x * rows, rows)
    slab_row = row_index(span)
    choices = [[], [], []]
    for at, (d, ranks) in enumerate(entries):
        place = first + span * d + slab_row
        if ranks is not None:
            place = jnp.where(among(rank_x, ranks), place, -1)
        choices[d % 3].append((at, (place >= 0) & (place < rows)))
    for field in range(fields):
        tiles = []
        for tile in range(3):
            kinds = []
            for options in choices:
                value = jnp.zeros((span, LANES), F32)
                for at, inside in options:
                    slab = refs[tile * len(entries) + at]
                    value = jnp.where(inside, slab[span * field : span * (field + 1), :], value)
                kinds.append(value)
            tiles.append(jnp.concatenate(kinds, axis=0))
        moved = pltpu.roll(jnp.concatenate(tiles, axis=1), row_shift, 0)
        fed_back = pltpu.roll(moved, shift, 1)
        merged[field, 0] = jnp.where(covered, fed_back, parent_next[field, 0])


def spread_matrix(columns):
    span = columns // 3
    matrix = np.zeros((2 * LANES, columns + LANES), np.float32)

    def source(m):
        return LANES if m < 0 else (LANES + 1 if m >= span else m)

    for c in range(-2, columns + 2):
        m, j = divmod(c, 3)
        at = c % (columns + LANES)
        if j == 0:
            matrix[source(m - 1), at] += 1.0
            matrix[source(m), at] += 2.0
        elif j == 1:
            matrix[source(m), at] += 3.0
        else:
            matrix[source(m), at] += 2.0
            matrix[source(m + 1), at] += 1.0
    return jnp.asarray(matrix, jnp.bfloat16)


def gather_matrix(columns):
    matrix = np.zeros((columns, columns // 3), np.float32)
    matrix[np.arange(columns), np.arange(columns) // 3] = 1.0
    return jnp.asarray(matrix, jnp.bfloat16)


def row_routes(size, rows):
    span = rows // 3
    starts = {}
    for start in range(size * (rows - span) - 2):
        for nest in range(size):
            for owner in {(start + span * nest) // rows, (start + span * nest + span + 1) // rows}:
                starts.setdefault((owner, nest), []).append(start)
    usual, rare, limits = {}, {}, [0, size * rows]
    for (owner, nest), needed in sorted(starts.items()):
        if owner == nest:
            continue
        if len(needed) > span:
            usual.setdefault(nest - owner, []).append((owner, nest))
        else:
            rare.setdefault(nest - owner, []).append((owner, nest))
            if needed[0] == 0:
                limits[0] = max(limits[0], needed[-1] + 2)
            else:
                limits[1] = min(limits[1], needed[0] + 1)
    return usual, rare, limits


def column_routes(size):
    routes = {}
    for k in (0, 1, -2, 2, -1):
        pairs = [(size // 2 + p, 3 * p + k) for p in range(size - size // 2)]
        routes[k] = [(s, n) for s, n in pairs if 0 <= n < size]
    return routes


def backward(pairs):
    return [(n, s) for s, n in pairs]


def per_device(
    parent_fields,
    parent_velocity,
    parent_mixing,
    nest_fields,
    nest_velocity,
    nest_mixing,
    nest_anchor,
):
    fields, levels, rows, columns = shape = parent_fields.shape
    channels = fields * levels
    span, last = rows // 3, columns // LANES - 1
    gx, gy = lax.axis_size("gx"), lax.axis_size("gy")
    height, width = rows + 8, columns + LANES
    pf = parent_fields.reshape(channels, rows, columns)
    nf = nest_fields.reshape(channels, rows, columns)
    nv = nest_velocity.reshape(2 * levels, rows, columns)
    nm = nest_mixing
    anchor = (nest_anchor, pl.BlockSpec(memory_space=pltpu.SMEM))

    def row_blocks(array):
        size = (array.shape[0], 8, columns)
        return [(array, block(size, (0, 0, 0))), (array, block(size, (0, rows // 8 - 1, 0)))]

    def column_blocks(array):
        size = (array.shape[0], rows, LANES)
        return [(array, block(size, (0, 0, 0))), (array, block(size, (0, 0, last)))]

    def shaped(*size):
        return size, block(size, (0,) * len(size))

    def whole_of(arrays):
        return [(array, whole(array)) for array in arrays]

    halo_rows = 4 * channels + 6 * levels
    rows_next, rows_prev, cols_next, cols_prev = call(
        pack_kernel,
        1,
        row_blocks(pf) + column_blocks(pf) + row_blocks(nf) + row_blocks(nv) + row_blocks(nm),
        [shaped(halo_rows, columns)] * 2 + [shaped(rows, LANES)] * 2,
    )
    top, bottom = halo_exchange("gx", rows_next, rows_prev)
    left, right = halo_exchange("gy", cols_next, cols_prev)

    usual, rare, limits = row_routes(gx, rows)
    rarely = (nest_anchor[0] < limits[0]) | (nest_anchor[0] >= limits[1])
    cuts = ((0, 3),)
    message_rows = -(-((span + 2) * (channels + 1)) // 16) * 16
    parent_next, *slabs = call(
        functools.partial(parent_kernel, cuts),
        levels,
        [
            anchor,
            (parent_fields, by_level(shape, 1)),
            (parent_velocity, by_level(parent_velocity.shape, 1)),
            (parent_mixing, by_level(parent_mixing.shape, 0)),
        ]
        + whole_of([top, bottom, left, right]),
        [(shape, by_level(shape, 1))]
        + [shaped(message_rows, LANES * (high - low)) for low, high in cuts for _ in range(3)],
        scratch=[(3, rows, LANES)],
    )
    nest_cols_next, nest_cols_prev = call(
        nest_columns_kernel,
        1,
        column_blocks(nf) + column_blocks(nv) + column_blocks(nm) + whole_of([top, bottom]),
        [shaped(height, LANES)] * 2,
    )
    nest_left, nest_right = halo_exchange("gy", nest_cols_next, nest_cols_prev)
    coefs, moved, weights = call(
        nest_start_kernel,
        levels,
        [
            (nest_fields, by_level(shape, 1)),
            (nest_velocity, by_level(nest_velocity.shape, 1)),
            (nest_mixing, by_level(nest_mixing.shape, 0)),
        ]
        + whole_of([top, bottom, nest_left, nest_right]),
        [
            ((levels, 5, height, width), by_level((levels, 5, height, width), 0)),
            ((levels, fields, height, width), by_level((levels, fields, height, width), 0)),
            shaped(height, width),
        ],
        scratch=[(fields + 3, height, width)],
    )

    entries = [(0, None)]
    entries += [(d, [n for _, n in pairs]) for d, pairs in usual.items()]
    entries += [(d, [n for _, n in pairs]) for d, pairs in rare.items()]
    messages = []
    for cut, (low, high) in enumerate(cuts):
        kinds = slabs[3 * cut : 3 * cut + 3]
        common = [lax.ppermute(kinds[d % 3], "gx", pairs) for d, pairs in usual.items()]
        others = lax.cond(
            rarely,
            lambda *kinds: [lax.ppermute(kinds[d % 3], "gx", pairs) for d, pairs in rare.items()],
            lambda *kinds: [kinds[d % 3] for d in rare],
            *kinds,
        )
        messages += call(
            functools.partial(row_select_kernel, entries, rows, channels),
            1,
            [anchor] + whole_of([kinds[0], *common, *others]),
            [shaped(message_rows, LANES)] * (high - low),
        )
    columns_of = column_routes(gy)
    ks = tuple(columns_of)
    received = [lax.ppermute(messages[k % 3], "gy", columns_of[k]) for k in ks]
    nest_result, coarse = call(
        functools.partial(nest_kernel, ks),
        levels,
        [anchor]
        + whole_of([spread_matrix(columns), gather_matrix(columns)])
        + [(coefs, by_level(coefs.shape, 0)), (moved, by_level(moved.shape, 0))]
        + whole_of([weights, *received]),
        [
            (shape, by_level(shape, 1)),
            (
                (span * channels, LANES),
                pl.BlockSpec((span * fields, LANES), lambda level: (level, 0)),
            ),
        ],
        scratch=[
            (message_rows, 2 * LANES),
            (message_rows, width),
            (fields, width // LANES, height, LANES),
            (fields, height, width),
            (span * fields, columns),
            (fields, columns // LANES, rows, LANES),
        ],
    )

    returned = {k: lax.ppermute(coarse, "gy", backward(columns_of[k])) for k in ks}
    placed = [returned[0]]
    for tile in (1, 2):
        own, other = returned[tile], returned[tile - 3]
        placed += call(
            functools.partial(column_select_kernel, tile, columns),
            1,
            [anchor] + whole_of([own, other]),
            [shaped(span * channels, LANES)],
        )
    common = [
        [lax.ppermute(tile, "gx", backward(pairs)) for pairs in usual.values()] for tile in placed
    ]
    others = lax.cond(
        rarely,
        lambda *tiles: [
            [lax.ppermute(tile, "gx", backward(pairs)) for pairs in rare.values()] for tile in tiles
        ],
        lambda *tiles: [[tile for _ in rare] for tile in tiles],
        *placed,
    )
    entries = [(0, None)]
    entries += [(d, [s for s, _ in pairs]) for d, pairs in usual.items()]
    entries += [(d, [s for s, _ in pairs]) for d, pairs in rare.items()]
    slab_block = pl.BlockSpec((span * fields, LANES), lambda level: (level, 0))
    slabs = [
        (array, slab_block)
        for tile in range(3)
        for array in (placed[tile], *common[tile], *others[tile])
    ]
    merged = call(
        functools.partial(merge_kernel, entries),
        levels,
        [anchor, (parent_next, by_level(shape, 1))] + slabs,
        [(shape, by_level(shape, 1))],
    )[0]
    return merged, nest_result


def solution(mesh):
    placed = (
        P(None, None, "gx", "gy"),
        P(None, None, "gx", "gy"),
        P(None, "gx", "gy"),
        P(None, None, "gx", "gy"),
        P(None, None, "gx", "gy"),
        P(None, "gx", "gy"),
        P(),
    )
    return jax.shard_map(
        per_device,
        mesh=mesh,
        in_specs=placed,
        out_specs=(P(None, None, "gx", "gy"), P(None, None, "gx", "gy")),
        check_vma=False,
    )
```

time: 558 us -> 132 us (0.24); the launches traced: 547 us -> 131 us
  local copies, waits for them, and re-layouts: 225 us -> 12.9 us
  other arithmetic: 126 us -> 0 us
  waiting for transfers between devices: 131 us -> 14 us
  Pallas kernels: 0 us -> 35.2 us
  starting transfers between devices: 61.4 us -> 67.5 us
    all_to_all x4 -> x0, waiting for transfers between devices: 121 us -> none  [the longest x2 97.7 us: per_device(): lax.all_to_all(outgoing, 'gy', split_axis=3, concat_axis=3, tiled=True)]
    reshape x2 -> x0, local copies, waits for them, and re-layouts: 65.1 us -> none  [the longest x1 61.7 us: block_mean(): state.reshape(extent[0], extent[1], extent[2] // 3, 3, extent[3] // 3, 3)]
    unnamed x38 -> x64, local copies, waits for them, and re-layouts: 54.3 us -> 6.27 us
    gather x4 -> x0, local copies, waits for them, and re-layouts: 36.8 us -> none  [the longest x2 29.5 us: take_columns(): jnp.take(values, jnp.clip(positions, 0, values.shape[3] - 1), axis=3)]
    pallas_call x0 -> x9, Pallas kernels: none -> 35.2 us  [call(): pl.pallas_call(body, grid=(grid,), out_shape=[jax.ShapeDtypeStruct(shape,...]
    reduce_sum x3 -> x0, other arithmetic: 29.9 us -> none  [the longest x1 20.5 us: block_mean(): return jnp.sum(grouped, axis=(3, 5)) / 9.0]
    ppermute x16 -> x32, starting transfers between devices: 41.6 us -> 67.5 us  [the longest x12 24.5 us: per_device(): lax.ppermute(tile, 'gx', backward(pairs))]
    select_n x11 -> x0, other arithmetic: 24.6 us -> none  [the longest x1 6.74 us: spread_columns(): return jnp.where(owner_mask(owners, count), tiled, 0.0)]
  transfers between devices with their start and end apart: 20 -> 32, of which waited for: 10 -> 5; matrix products, arithmetic and copies ran while one was open for 18% -> 2% of each run, Pallas kernels for 0% -> 10%
where the time goes in v2:
time: 132 us; the launch traced here: 131 us
  starting transfers between devices  67.5 us (51%)
  Pallas kernels  35.2 us (27%)
  waiting for transfers between devices  14 us (11%)
  local copies, waits for them, and re-layouts  12.9 us (10%)
  between operations  1.45 us (1%)
    pallas_call x9, Pallas kernels, call(): pl.pallas_call(body, grid=(grid,), out_shape=[jax.ShapeDtypeStruct(shape,...  35.2 us
    ppermute x12, starting transfers between devices, per_device(): lax.ppermute(tile, 'gx', backward(pairs))  24.5 us
    ppermute x5, starting transfers between devices, per_device(): lax.ppermute(coarse, 'gy', backward(columns_of[k]))  13.2 us
    ppermute x3, starting transfers between devices, halo_exchange(): lax.ppermute(to_next, axis, [(i, i + 1) for i in range(ends)])  11.7 us
    ppermute x4, starting transfers between devices, per_device(): lax.ppermute(kinds[d % 3], 'gx', pairs)  9.63 us
    cond x8, local copies, waits for them, and re-layouts  6.67 us
    unnamed x64, local copies, waits for them, and re-layouts  6.27 us
    ppermute x5, waiting for transfers between devices, per_device(): received = [lax.ppermute(messages[k % 3], 'gy', columns_of[k]) for k in ks]  5.35 us
  transfers between devices with their start and end apart: 32, of which 5 were waited for; matrix products, arithmetic and copies ran while one was open for 2% of the time, Pallas kernels for 10%

profile of v2, /device:TPU:1, one launch (start us, length us, event | category | flops | bytes accessed | tf_op | source)
XLA Modules:
  0.0 131.1 jit_solution(12281851388313242060)
XLA Ops:
  0.6 2.6 %shard_map.104 = (f32[104,384]{1,0:T(8,128)}, f32[104,384]{1,0:T(8,128)}, f32[48,128]{1,0:T(8,128)}, f32[48,128]{1,0:T(8,128)}) custom-call(f32[20,48,384]{2,1,0:T(8,128)} %bitcast.5, f32[20,48,384]{2,1,0:T(8,128)} %bitcast.6, f32[20,48,384]{2,1,0:T(8,128)} %bitcast.7, f32[20,48,384]{2,1,0:T(8,128)} %bitcast.8, f32[20,48,384]{2,1,0:T(8,128)} %bitcast.9, ...), custom_call_target="tpu_custom_call" | custom-call | tf_op jit(solution)/shard_map/pallas_call | solution.py:33
  3.3 4.5 %collective-permute-start.8 = (f32[104,384]{1,0:T(8,128)}, f32[104,384]{1,0:T(8,128)S(1)}, u32[]{:S(2)}, u32[]{:S(2)}) collective-permute-start(f32[104,384]{1,0:T(8,128)} %get-tuple-element.56), channel_id=1, source_target_pairs={{0,8},{8,16},{16,24},{1,9},{9,17},{17,25},{2,10},{10,18},{18,26},{... | collective-permute-start | bytes 479240 | tf_op jit(solution)/shard_map/ppermute | solution.py:62
  7.8 1.9 %collective-permute-start.9 = (f32[104,384]{1,0:T(8,128)}, f32[104,384]{1,0:T(8,128)S(1)}, u32[]{:S(2)}, u32[]{:S(2)}) collective-permute-start(f32[104,384]{1,0:T(8,128)} %get-tuple-element.57), channel_id=1, source_target_pairs={{8,0},{16,8},{24,16},{9,1},{17,9},{25,17},{10,2},{18,10},{26,18},{... | collective-permute-start | bytes 479240 | tf_op jit(solution)/shard_map/ppermute | solution.py:63
  9.7 3.1 %collective-permute-start.10 = (f32[48,128]{1,0:T(8,128)}, f32[48,128]{1,0:T(8,128)S(1)}, u32[]{:S(2)}, u32[]{:S(2)}) collective-permute-start(f32[48,128]{1,0:T(8,128)} %get-tuple-element.58), channel_id=1, source_target_pairs={{0,1},{1,2},{2,3},{3,4},{4,5},{5,6},{6,7},{8,9},{9,10},{10,11},{11... | collective-permute-start | bytes 73736 | tf_op jit(solution)/shard_map/ppermute | solution.py:62
  14.2 3.5 %collective-permute-done.11.right = f32[48,128]{1,0:T(8,128)S(1)} collective-permute-done((f32[48,128]{1,0:T(8,128)}, f32[48,128]{1,0:T(8,128)S(1)}, u32[]{:S(2)}, u32[]{:S(2)}) %collective-permute-start.11) | collective-permute-done | bytes 24608 | tf_op jit(solution)/shard_map/ppermute | solution.py:63
  19.0 6.9 %shard_map.105 = (f32[5,4,48,384]{3,2,1,0:T(8,128)}, f32[384,384]{1,0:T(8,128)}, f32[384,384]{1,0:T(8,128)}, f32[384,384]{1,0:T(8,128)S(1)}) custom-call(s32[2]{0:T(128)} %anchor.11, f32[5,4,48,384]{3,2,1,0:T(8,128)} %pf.1, f32[2,4,48,384]{3,2,1,0:T(8,128)} %pv.1, f32[4,48,384]{2,1,0:T(8,128)} %pm.1, f32[104,384]{1,0:T(8,128)} %copy-done, ...), custom_call_target="tpu_custom_call" | custom-call | tf_op jit(solution)/shard_map/pallas_call | solution.py:33
  26.7 5.7 %collective-permute-start.14 = (f32[384,384]{1,0:T(8,128)}, f32[384,384]{1,0:T(8,128)S(1)}, u32[]{:S(2)}, u32[]{:S(2)}) collective-permute-start(f32[384,384]{1,0:T(8,128)} %get-tuple-element.67), channel_id=1, source_target_pairs={{0,8},{8,16},{16,24},{1,9},{9,17},{17,25},{2,10},{10,18},{18,26},{... | collective-permute-start | bytes 1769480 | tf_op jit(solution)/shard_map/ppermute | solution.py:625
  33.7 2.7 %conditional.2 = (f32[384,384]{1,0:T(8,128)}, f32[384,384]{1,0:T(8,128)}) conditional(s32[]{:T(128)} %bitcast.3, (f32[384,384]{1,0:T(8,128)S(1)}, f32[384,384]{1,0:T(8,128)}) %tuple.23, (f32[384,384]{1,0:T(8,128)S(1)}, f32[384,384]{1,0:T(8,128)}) %tuple.23), branch_computations={%region_0.0_spmd, %region_1.0_spmd} | conditional | bytes 4718688 | solution.py:626
  38.4 2.9 %shard_map.106 = (f32[56,128]{1,0:T(8,128)}, f32[56,128]{1,0:T(8,128)}) custom-call(f32[20,48,384]{2,1,0:T(8,128)} %bitcast.11, f32[20,48,384]{2,1,0:T(8,128)} %bitcast.12, f32[8,48,384]{2,1,0:T(8,128)} %bitcast.15, f32[8,48,384]{2,1,0:T(8,128)} %bitcast.16, f32[4,48,384]{2,1,0:T(8,128)} %nm.1, f32[4,48,384]{2,1,0:T(8,128)} %nm.1, f32[104,384]{1,0:T(8,128)} %copy-done, ...), custom_call_target="tpu_custom_call" | custom-call | tf_op jit(solution)/shard_map/pallas_call | solution.py:33
  41.3 4.0 %collective-permute-start.12 = (f32[56,128]{1,0:T(8,128)}, f32[56,128]{1,0:T(8,128)S(1)}, u32[]{:S(2)}, u32[]{:S(2)}) collective-permute-start(f32[56,128]{1,0:T(8,128)} %get-tuple-element.61), channel_id=1, source_target_pairs={{0,1},{1,2},{2,3},{3,4},{4,5},{5,6},{6,7},{8,9},{9,10},{10,11},{11... | collective-permute-start | bytes 86024 | tf_op jit(solution)/shard_map/ppermute | solution.py:62
  48.5 3.2 %shard_map.108 = (f32[384,128]{1,0:T(8,128)}, f32[384,128]{1,0:T(8,128)}, f32[384,128]{1,0:T(8,128)}) custom-call(s32[2]{0:T(128)} %anchor.11, f32[384,384]{1,0:T(8,128)} %get-tuple-element.66.refs_0_, f32[384,384]{1,0:T(8,128)} %copy-done.3, f32[384,384]{1,0:T(8,128)} %copy-done.5, f32[384,384]{1,0:T(8,128)} %copy-done.4, f32[384,384]{1,0:T(8,128)} %copy-done.2, ...), custom_call_target="tpu_custom_call" | custom-call | tf_op jit(solution)/shard_map/pallas_call | solution.py:33
  55.7 5.6 %shard_map.107 = (f32[4,5,56,512]{3,2,1,0:T(8,128)}, f32[4,5,56,512]{3,2,1,0:T(8,128)}, f32[56,512]{1,0:T(8,128)}) custom-call(f32[5,4,48,384]{3,2,1,0:T(8,128)} %nf.1, f32[2,4,48,384]{3,2,1,0:T(8,128)} %nv.1, f32[4,48,384]{2,1,0:T(8,128)} %nm.1, f32[104,384]{1,0:T(8,128)} %copy-done, f32[104,384]{1,0:T(8,128)} %copy-done.1, f32[56,128]{1,0:T(8,128)} %copy-done.27, ...), custom_call_target="tpu_custom_call" | custom-call | tf_op jit(solution)/shard_map/pallas_call | solution.py:33
  61.3 5.3 %collective-permute-done.18.refs_0_ = f32[384,128]{1,0:T(8,128)S(1)} collective-permute-done((f32[384,128]{1,0:T(8,128)}, f32[384,128]{1,0:T(8,128)S(1)}, u32[]{:S(2)}, u32[]{:S(2)}) %collective-permute-start.18) | collective-permute-done | bytes 196640 | tf_op jit(solution)/shard_map/ppermute | solution.py:640
  67.6 7.5 %shard_map.109 = (f32[5,4,48,384]{3,2,1,0:T(8,128)}, f32[320,128]{1,0:T(8,128)}) custom-call(s32[2]{0:T(128)} %anchor.11, bf16[256,512]{1,0:T(8,128)(2,1)} %constant.10.clone.spread, bf16[384,128]{1,0:T(8,128)(2,1)} %constant.11.clone.gather, f32[4,5,56,512]{3,2,1,0:T(8,128)} %get-tuple-element.63.coefs, f32[4,5,56,512]{3,2,1,0:T(8,128)} %get-tuple-element.64.moved, ...), custom_call_target="tpu_custom_call" | custom-call | tf_op jit(solution)/shard_map/pallas_call | solution.py:33
  77.8 10.5 %collective-permute-start.23 = (f32[320,128]{1,0:T(8,128)}, f32[320,128]{1,0:T(8,128)S(1)}, u32[]{:S(2)}, u32[]{:S(2)}) collective-permute-start(f32[320,128]{1,0:T(8,128)} %get-tuple-element.74), channel_id=1, source_target_pairs={{0,4},{3,5},{6,6},{8,12},{11,13},{14,14},{16,20},{19,21},{22,22},{... | collective-permute-start | bytes 491528 | tf_op jit(solution)/shard_map/ppermute | solution.py:665
  93.1 4.0 %conditional.3 = (f32[320,128]{1,0:T(8,128)}, f32[320,128]{1,0:T(8,128)}, f32[320,128]{1,0:T(8,128)}, f32[320,128]{1,0:T(8,128)}, f32[320,128]{1,0:T(8,128)}, /*index=5*/f32[320,128]{1,0:T(8,128)}) conditional(s32[]{:T(128)} %bitcast.3, (f32[320,128]{1,0:T(8,128)S(1)}, f32[320,128]{1,0:T(8,128)S(1)}, f32[320,128]{1,0:T(8,128)S(1)}) %tuple.24, ...), branch_computations={%region_2.0_spmd, %region_3.0_spmd} | conditional | bytes 3932448 | solution.py:678
  99.0 5.1 %collective-permute-start.37 = (f32[320,128]{1,0:T(8,128)S(1)}, f32[320,128]{1,0:T(8,128)S(1)}, u32[]{:S(2)}, u32[]{:S(2)}) collective-permute-start(f32[320,128]{1,0:T(8,128)S(1)} %shard_map.111.refs_14_), channel_id=1, source_target_pairs={{0,8},{8,16},{16,24},{1,9},{9,17},{17,25},{2,10},{10,18},{18,26},{... | collective-permute-start | bytes 491528 | tf_op jit(solution)/shard_map/ppermute | solution.py:676
  104.2 2.3 %collective-permute-start.36 = (f32[320,128]{1,0:T(8,128)S(1)}, f32[320,128]{1,0:T(8,128)S(1)}, u32[]{:S(2)}, u32[]{:S(2)}) collective-permute-start(f32[320,128]{1,0:T(8,128)S(1)} %shard_map.111.refs_14_), channel_id=1, source_target_pairs={{8,0},{16,8},{24,16},{9,1},{17,9},{25,17},{10,2},{18,10},{26,18},{... | collective-permute-start | bytes 491528 | tf_op jit(solution)/shard_map/ppermute | solution.py:676
  108.5 3.2 %collective-permute-start.33 = (f32[320,128]{1,0:T(8,128)S(1)}, f32[320,128]{1,0:T(8,128)S(1)}, u32[]{:S(2)}, u32[]{:S(2)}) collective-permute-start(f32[320,128]{1,0:T(8,128)S(1)} %shard_map.110.refs_7_), channel_id=1, source_target_pairs={{0,8},{8,16},{16,24},{1,9},{9,17},{17,25},{2,10},{10,18},{18,26},{... | collective-permute-start | bytes 491528 | tf_op jit(solution)/shard_map/ppermute | solution.py:676
  111.8 2.3 %collective-permute-start.32 = (f32[320,128]{1,0:T(8,128)S(1)}, f32[320,128]{1,0:T(8,128)S(1)}, u32[]{:S(2)}, u32[]{:S(2)}) collective-permute-start(f32[320,128]{1,0:T(8,128)S(1)} %shard_map.110.refs_7_), channel_id=1, source_target_pairs={{8,0},{16,8},{24,16},{9,1},{17,9},{25,17},{10,2},{18,10},{26,18},{... | collective-permute-start | bytes 491528 | tf_op jit(solution)/shard_map/ppermute | solution.py:676
  116.2 3.2 %collective-permute-start.25 = (f32[320,128]{1,0:T(8,128)S(1)}, f32[320,128]{1,0:T(8,128)S(1)}, u32[]{:S(2)}, u32[]{:S(2)}) collective-permute-start(f32[320,128]{1,0:T(8,128)S(1)} %collective-permute-done.23.refs_0_), channel_id=1, source_target_pairs={{0,8},{8,16},{16,24},{1,9},{9,17},{17,25},{2,10},{10,18},{18,26},{... | collective-permute-start | bytes 491528 | tf_op jit(solution)/shard_map/ppermute | solution.py:676
  119.4 2.3 %collective-permute-start.24 = (f32[320,128]{1,0:T(8,128)S(1)}, f32[320,128]{1,0:T(8,128)S(1)}, u32[]{:S(2)}, u32[]{:S(2)}) collective-permute-start(f32[320,128]{1,0:T(8,128)S(1)} %collective-permute-done.23.refs_0_), channel_id=1, source_target_pairs={{8,0},{16,8},{24,16},{9,1},{17,9},{25,17},{10,2},{18,10},{26,18},{... | collective-permute-start | bytes 491528 | tf_op jit(solution)/shard_map/ppermute | solution.py:676
  122.0 4.1 %collective-permute-done.24.refs_1_ = f32[320,128]{1,0:T(8,128)S(1)} collective-permute-done((f32[320,128]{1,0:T(8,128)S(1)}, f32[320,128]{1,0:T(8,128)S(1)}, u32[]{:S(2)}, u32[]{:S(2)}) %collective-permute-start.24) | collective-permute-done | bytes 163872 | tf_op jit(solution)/shard_map/ppermute | solution.py:676
  126.7 4.4 %shard_map.112 = f32[5,4,48,384]{3,2,1,0:T(8,128)} custom-call(s32[2]{0:T(128)} %anchor.11, f32[5,4,48,384]{3,2,1,0:T(8,128)} %get-tuple-element.60.parent_next, f32[320,128]{1,0:T(8,128)S(1)} %collective-permute-done.23.refs_0_, f32[320,128]{1,0:T(8,128)} %copy-done.22, f32[320,128]{1,0:T(8,128)} %copy-done.21, f32[320,128]{1,0:T(8,128)} %copy-done.20, ...), custom_call_target="tpu_custom_call" | custom-call | tf_op jit(solution)/shard_map/pallas_call | solution.py:33
  (123 shorter events, 35.2 us)
Async XLA Ops:
  3.3 14.4 %collective-permute-start.8 = (f32[104,384]{1,0:T(8,128)}, f32[104,384]{1,0:T(8,128)S(1)}, u32[]{:S(2)}, u32[]{:S(2)}) collective-permute-start(f32[104,384]{1,0:T(8,128)} %get-tuple-element.56), channel_id=1, source_target_pairs={{0,8},{8,16},{16,24},{1,9},{9,17},{17,25},{2,10},{10,18},{18,26},{... | collective-permute-start | bytes 479240 | tf_op jit(solution)/shard_map/ppermute | solution.py:62
  7.8 9.9 %collective-permute-start.9 = (f32[104,384]{1,0:T(8,128)}, f32[104,384]{1,0:T(8,128)S(1)}, u32[]{:S(2)}, u32[]{:S(2)}) collective-permute-start(f32[104,384]{1,0:T(8,128)} %get-tuple-element.57), channel_id=1, source_target_pairs={{8,0},{16,8},{24,16},{9,1},{17,9},{25,17},{10,2},{18,10},{26,18},{... | collective-permute-start | bytes 479240 | tf_op jit(solution)/shard_map/ppermute | solution.py:63
  25.9 19.5 %collective-permute-start.17 = (f32[384,384]{1,0:T(8,128)}, f32[384,384]{1,0:T(8,128)S(1)}, u32[]{:S(2)}, u32[]{:S(2)}) collective-permute-start(f32[384,384]{1,0:T(8,128)} %get-tuple-element.67), channel_id=1, source_target_pairs={{16,0},{17,1},{18,2},{19,3},{20,4},{21,5},{22,6},{23,7}} | collective-permute-start | bytes 1769480 | tf_op jit(solution)/shard_map/ppermute | solution.py:625
  26.7 20.0 %collective-permute-start.14 = (f32[384,384]{1,0:T(8,128)}, f32[384,384]{1,0:T(8,128)S(1)}, u32[]{:S(2)}, u32[]{:S(2)}) collective-permute-start(f32[384,384]{1,0:T(8,128)} %get-tuple-element.67), channel_id=1, source_target_pairs={{0,8},{8,16},{16,24},{1,9},{9,17},{17,25},{2,10},{10,18},{18,26},{... | collective-permute-start | bytes 1769480 | tf_op jit(solution)/shard_map/ppermute | solution.py:625
  32.4 14.3 %collective-permute-start.16 = (f32[384,384]{1,0:T(8,128)S(1)}, f32[384,384]{1,0:T(8,128)S(1)}, u32[]{:S(2)}, u32[]{:S(2)}) collective-permute-start(f32[384,384]{1,0:T(8,128)S(1)} %get-tuple-element.68), channel_id=1, source_target_pairs={{8,24},{9,25},{10,26},{11,27},{12,28},{13,29},{14,30},{15,31}} | collective-permute-start | bytes 1769480 | tf_op jit(solution)/shard_map/ppermute | solution.py:625
  36.5 11.2 %collective-permute-start.15 = (f32[384,384]{1,0:T(8,128)S(1)}, f32[384,384]{1,0:T(8,128)S(1)}, u32[]{:S(2)}, u32[]{:S(2)}) collective-permute-start(f32[384,384]{1,0:T(8,128)S(1)} %get-tuple-element.68), channel_id=1, source_target_pairs={{8,0},{16,8},{24,16},{9,1},{17,9},{25,17},{10,2},{18,10},{26,18},{... | collective-permute-start | bytes 1769480 | tf_op jit(solution)/shard_map/ppermute | solution.py:625
  41.3 13.0 %collective-permute-start.12 = (f32[56,128]{1,0:T(8,128)}, f32[56,128]{1,0:T(8,128)S(1)}, u32[]{:S(2)}, u32[]{:S(2)}) collective-permute-start(f32[56,128]{1,0:T(8,128)} %get-tuple-element.61), channel_id=1, source_target_pairs={{0,1},{1,2},{2,3},{3,4},{4,5},{5,6},{6,7},{8,9},{9,10},{10,11},{11... | collective-permute-start | bytes 86024 | tf_op jit(solution)/shard_map/ppermute | solution.py:62
  45.4 9.6 %collective-permute-start.13 = (f32[56,128]{1,0:T(8,128)}, f32[56,128]{1,0:T(8,128)S(1)}, u32[]{:S(2)}, u32[]{:S(2)}) collective-permute-start(f32[56,128]{1,0:T(8,128)} %get-tuple-element.62), channel_id=1, source_target_pairs={{1,0},{2,1},{3,2},{4,3},{5,4},{6,5},{7,6},{9,8},{10,9},{11,10},{12... | collective-permute-start | bytes 86024 | tf_op jit(solution)/shard_map/ppermute | solution.py:63
  51.7 15.0 %collective-permute-start.20 = (f32[384,128]{1,0:T(8,128)}, f32[384,128]{1,0:T(8,128)S(1)}, u32[]{:S(2)}, u32[]{:S(2)}) collective-permute-start(f32[384,128]{1,0:T(8,128)} %get-tuple-element.72), channel_id=1, source_target_pairs={{5,1},{6,4},{7,7},{13,9},{14,12},{15,15},{21,17},{22,20},{23,23},{... | collective-permute-start | bytes 589832 | tf_op jit(solution)/shard_map/ppermute | solution.py:640
  52.3 14.3 %collective-permute-start.19 = (f32[384,128]{1,0:T(8,128)}, f32[384,128]{1,0:T(8,128)S(1)}, u32[]{:S(2)}, u32[]{:S(2)}) collective-permute-start(f32[384,128]{1,0:T(8,128)} %get-tuple-element.72), channel_id=1, source_target_pairs={{4,1},{5,4},{6,7},{12,9},{13,12},{14,15},{20,17},{21,20},{22,23},{... | collective-permute-start | bytes 589832 | tf_op jit(solution)/shard_map/ppermute | solution.py:640
  53.0 13.6 %collective-permute-start.18 = (f32[384,128]{1,0:T(8,128)}, f32[384,128]{1,0:T(8,128)S(1)}, u32[]{:S(2)}, u32[]{:S(2)}) collective-permute-start(f32[384,128]{1,0:T(8,128)} %get-tuple-element.71), channel_id=1, source_target_pairs={{4,0},{5,3},{6,6},{12,8},{13,11},{14,14},{20,16},{21,19},{22,22},{... | collective-permute-start | bytes 589832 | tf_op jit(solution)/shard_map/ppermute | solution.py:640
  54.3 12.3 %collective-permute-start.22 = (f32[384,128]{1,0:T(8,128)}, f32[384,128]{1,0:T(8,128)S(1)}, u32[]{:S(2)}, u32[]{:S(2)}) collective-permute-start(f32[384,128]{1,0:T(8,128)} %get-tuple-element.73), channel_id=1, source_target_pairs={{5,2},{6,5},{13,10},{14,13},{21,18},{22,21},{29,26},{30,29}} | collective-permute-start | bytes 589832 | tf_op jit(solution)/shard_map/ppermute | solution.py:640
  55.0 11.7 %collective-permute-start.21 = (f32[384,128]{1,0:T(8,128)}, f32[384,128]{1,0:T(8,128)S(1)}, u32[]{:S(2)}, u32[]{:S(2)}) collective-permute-start(f32[384,128]{1,0:T(8,128)} %get-tuple-element.73), channel_id=1, source_target_pairs={{4,2},{5,5},{12,10},{13,13},{20,18},{21,21},{28,26},{29,29}} | collective-permute-start | bytes 589832 | tf_op jit(solution)/shard_map/ppermute | solution.py:640
  75.1 13.3 %collective-permute-start.31 = (f32[320,128]{1,0:T(8,128)}, f32[320,128]{1,0:T(8,128)S(1)}, u32[]{:S(2)}, u32[]{:S(2)}) collective-permute-start(f32[320,128]{1,0:T(8,128)} %get-tuple-element.74), channel_id=1, source_target_pairs={{2,5},{5,6},{10,13},{13,14},{18,21},{21,22},{26,29},{29,30}} | collective-permute-start | bytes 491528 | tf_op jit(solution)/shard_map/ppermute | solution.py:665
  75.8 12.6 %collective-permute-start.30 = (f32[320,128]{1,0:T(8,128)}, f32[320,128]{1,0:T(8,128)S(1)}, u32[]{:S(2)}, u32[]{:S(2)}) collective-permute-start(f32[320,128]{1,0:T(8,128)} %get-tuple-element.74), channel_id=1, source_target_pairs={{2,4},{5,5},{10,12},{13,13},{18,20},{21,21},{26,28},{29,29}} | collective-permute-start | bytes 491528 | tf_op jit(solution)/shard_map/ppermute | solution.py:665
  76.5 14.3 %collective-permute-start.29 = (f32[320,128]{1,0:T(8,128)}, f32[320,128]{1,0:T(8,128)S(1)}, u32[]{:S(2)}, u32[]{:S(2)}) collective-permute-start(f32[320,128]{1,0:T(8,128)} %get-tuple-element.74), channel_id=1, source_target_pairs={{1,5},{4,6},{7,7},{9,13},{12,14},{15,15},{17,21},{20,22},{23,23},{... | collective-permute-start | bytes 491528 | tf_op jit(solution)/shard_map/ppermute | solution.py:665
  77.1 13.6 %collective-permute-start.28 = (f32[320,128]{1,0:T(8,128)}, f32[320,128]{1,0:T(8,128)S(1)}, u32[]{:S(2)}, u32[]{:S(2)}) collective-permute-start(f32[320,128]{1,0:T(8,128)} %get-tuple-element.74), channel_id=1, source_target_pairs={{1,4},{4,5},{7,6},{9,12},{12,13},{15,14},{17,20},{20,21},{23,22},{... | collective-permute-start | bytes 491528 | tf_op jit(solution)/shard_map/ppermute | solution.py:665
  77.8 15.3 %collective-permute-start.23 = (f32[320,128]{1,0:T(8,128)}, f32[320,128]{1,0:T(8,128)S(1)}, u32[]{:S(2)}, u32[]{:S(2)}) collective-permute-start(f32[320,128]{1,0:T(8,128)} %get-tuple-element.74), channel_id=1, source_target_pairs={{0,4},{3,5},{6,6},{8,12},{11,13},{14,14},{16,20},{19,21},{22,22},{... | collective-permute-start | bytes 491528 | tf_op jit(solution)/shard_map/ppermute | solution.py:665
  97.1 10.1 %collective-permute-start.39 = (f32[320,128]{1,0:T(8,128)S(1)}, f32[320,128]{1,0:T(8,128)S(1)}, u32[]{:S(2)}, u32[]{:S(2)}) collective-permute-start(f32[320,128]{1,0:T(8,128)S(1)} %shard_map.111.refs_14_), channel_id=1, source_target_pairs={{0,16},{1,17},{2,18},{3,19},{4,20},{5,21},{6,22},{7,23}} | collective-permute-start | bytes 491528 | tf_op jit(solution)/shard_map/ppermute | solution.py:676
  97.7 10.8 %collective-permute-start.38 = (f32[320,128]{1,0:T(8,128)S(1)}, f32[320,128]{1,0:T(8,128)S(1)}, u32[]{:S(2)}, u32[]{:S(2)}) collective-permute-start(f32[320,128]{1,0:T(8,128)S(1)} %shard_map.111.refs_14_), channel_id=1, source_target_pairs={{24,8},{25,9},{26,10},{27,11},{28,12},{29,13},{30,14},{31,15}} | collective-permute-start | bytes 491528 | tf_op jit(solution)/shard_map/ppermute | solution.py:676
  99.0 12.7 %collective-permute-start.37 = (f32[320,128]{1,0:T(8,128)S(1)}, f32[320,128]{1,0:T(8,128)S(1)}, u32[]{:S(2)}, u32[]{:S(2)}) collective-permute-start(f32[320,128]{1,0:T(8,128)S(1)} %shard_map.111.refs_14_), channel_id=1, source_target_pairs={{0,8},{8,16},{16,24},{1,9},{9,17},{17,25},{2,10},{10,18},{18,26},{... | collective-permute-start | bytes 491528 | tf_op jit(solution)/shard_map/ppermute | solution.py:676
  104.2 9.9 %collective-permute-start.36 = (f32[320,128]{1,0:T(8,128)S(1)}, f32[320,128]{1,0:T(8,128)S(1)}, u32[]{:S(2)}, u32[]{:S(2)}) collective-permute-start(f32[320,128]{1,0:T(8,128)S(1)} %shard_map.111.refs_14_), channel_id=1, source_target_pairs={{8,0},{16,8},{24,16},{9,1},{17,9},{25,17},{10,2},{18,10},{26,18},{... | collective-permute-start | bytes 491528 | tf_op jit(solution)/shard_map/ppermute | solution.py:676
  108.5 10.9 %collective-permute-start.33 = (f32[320,128]{1,0:T(8,128)S(1)}, f32[320,128]{1,0:T(8,128)S(1)}, u32[]{:S(2)}, u32[]{:S(2)}) collective-permute-start(f32[320,128]{1,0:T(8,128)S(1)} %shard_map.110.refs_7_), channel_id=1, source_target_pairs={{0,8},{8,16},{16,24},{1,9},{9,17},{17,25},{2,10},{10,18},{18,26},{... | collective-permute-start | bytes 491528 | tf_op jit(solution)/shard_map/ppermute | solution.py:676
  111.8 10.0 %collective-permute-start.32 = (f32[320,128]{1,0:T(8,128)S(1)}, f32[320,128]{1,0:T(8,128)S(1)}, u32[]{:S(2)}, u32[]{:S(2)}) collective-permute-start(f32[320,128]{1,0:T(8,128)S(1)} %shard_map.110.refs_7_), channel_id=1, source_target_pairs={{8,0},{16,8},{24,16},{9,1},{17,9},{25,17},{10,2},{18,10},{26,18},{... | collective-permute-start | bytes 491528 | tf_op jit(solution)/shard_map/ppermute | solution.py:676
  (40 other events, 204.6 us)
